TPU v7x, 32 devices: a whole 2x2x4 slice. The times are simulated.
32 devices in a mesh: mpo: 4 (over z), sec: 8 (over y, x, core).
Axes of the slice: x: 2, y: 2, z: 4, core: 2. Of those that a mesh axis runs over, the one named last changes fastest.
Arguments:
- wavefunction: bfloat16 [2, 64, 512, 512], P(None, 'sec'), may hold values from -6 to 6
- left_env: bfloat16 [8, 64, 512, 512], P('mpo', 'sec'), may hold values from -0.25 to 0.25
- right_env: bfloat16 [8, 64, 512, 512], P('mpo', 'sec'), may hold values from -0.09375 to 0.09375
- block_dims: int32 [64], P('sec'), may hold values from 128 to 512, as said below
- mpo_shift: int32 [8], P('mpo'), may hold values from -1 to 1
Outputs:
- sigma_blocks: bfloat16 [2, 64, 512, 512], P(None, 'sec', 'mpo')
Inputs may be any that keep to these rules, and one draw needn't show every extreme that they name: `block_dims`: some block is full.
All inputs are finite; a program needn't handle non-finite values.
Results may differ from a plain program's by a relative error of at most 0.0049.
Values may be sent and summed in bfloat16 or wider, within the bound.
No kernel may reach another device: no remote copies, remote signals or barrier semaphores. Data moves between devices by JAX's collectives and lax.ppermute only.
A program may use at most 192 MiB of HBM per device.

v0:
```python
import jax
import jax.numpy as jnp
from jax import lax
from jax.sharding import PartitionSpec as P


def shifted(block, axis, distance):
    devices = range(lax.axis_size(axis))
    route = [((i - distance) % len(devices), i) for i in devices]
    return lax.ppermute(block, axis, route)


def body(wavefunction, left_env, right_env, block_dims, mpo_shift):
    sec_count = lax.axis_size("sec")
    sec_index = lax.axis_index("sec")
    lower_raw = shifted(wavefunction, "sec", 1)
    upper_raw = shifted(wavefunction, "sec", -1)
    empty_block = jnp.zeros_like(wavefunction[:, :1])
    from_lower = jnp.where(
        sec_index == 0, jnp.concatenate([empty_block, lower_raw[:, :-1]], axis=1), lower_raw
    )
    from_upper = jnp.where(
        sec_index == sec_count - 1,
        jnp.concatenate([upper_raw[:, 1:], empty_block], axis=1),
        upper_raw,
    )
    variants = jnp.stack([from_upper, wavefunction, from_lower])
    left_parts = []
    for mpo_row in range(left_env.shape[0]):
        chosen = lax.dynamic_index_in_dim(variants, mpo_shift[mpo_row] + 1, 0, keepdims=False)
        left_parts.append(
            jnp.einsum(
                "sab,ksbc->ksac", left_env[mpo_row], chosen, preferred_element_type=jnp.float32
            ).astype(jnp.bfloat16)
        )
    accumulated = jnp.zeros(wavefunction.shape, jnp.float32)
    for mpo_row in range(left_env.shape[0]):
        accumulated = accumulated + jnp.einsum(
            "ksac,scd->ksad",
            left_parts[mpo_row],
            right_env[mpo_row],
            preferred_element_type=jnp.float32,
        )
    summed = lax.psum_scatter(accumulated, "mpo", scatter_dimension=2, tiled=True)
    slab_rows = summed.shape[2]
    row_index = lax.axis_index("mpo") * slab_rows + jnp.arange(slab_rows, dtype=jnp.int32)
    col_index = jnp.arange(summed.shape[3], dtype=jnp.int32)
    block_limit = block_dims[None, :, None, None]
    inside = (row_index[None, None, :, None] < block_limit) & (
        col_index[None, None, None, :] < block_limit
    )
    return jnp.where(inside, summed, jnp.zeros_like(summed)).astype(jnp.bfloat16)


def solution(mesh):
    placed = (
        P(None, "sec", None, None),
        P("mpo", "sec", None, None),
        P("mpo", "sec", None, None),
        P("sec"),
        P("mpo"),
    )
    return jax.shard_map(
        body, mesh=mesh, in_specs=placed, out_specs=P(None, "sec", "mpo", None), check_vma=False
    )
```

profile of v0, /device:TPU:0, one launch (start us, length us, event | category | flops | bytes accessed | tf_op | source)
XLA Modules:
  0.0 578.2 jit_solution(9596608527923404598)
XLA Ops:
  6.5 0.0 reduce-scatter.2.cloned.1.call-start
  6.5 3.3 collective-permute-start
  9.9 0.0 collective-permute-start.1
  9.9 1.3 fusion.32
  13.6 176.5 %collective-permute-done = bf16[2,8,512,512]{3,2,1,0:T(8,128)(2,1)} collective-permute-done((bf16[2,8,512,512]{3,2,1,0:T(8,128)(2,1)}, bf16[2,8,512,512]{3,2,1,0:T(8,128)(2,1)}, u32[]{:S(2)}, u32[]{:S(2)}) %collective-permute-start) | collective-permute-done | bytes 8388640 | tf_op jit(solution)/shard_map/ppermute | solution.py:10
  190.1 3.6 slice.32
  193.7 0.0 collective-permute-done.1
  193.7 6.6 %slice.33 = bf16[2,7,512,512]{3,2,1,0:T(8,128)(2,1)} slice(bf16[2,8,512,512]{3,2,1,0:T(8,128)(2,1)} %collective-permute-done.1), slice={[0:2], [0:7], [0:512], [0:512]} | slice | bytes 14680064 | tf_op jit(solution)/shard_map/slice | solution.py:20
  200.3 0.0 copy-start
  200.3 7.6 %select_bitcast_fusion.1 = bf16[1,2,8,512,512]{4,3,2,1,0:T(8,128)(2,1)} fusion(bf16[2,8,512,512]{3,2,1,0:T(8,128)(2,1)} %collective-permute-done, bf16[2,7,512,512]{3,2,1,0:T(8,128)(2,1)S(1)} %slice.32, pred[]{:T(512)S(6)} %eq.6), kind=kLoop, calls=%fused_computation.15 | loop fusion | flops 4194304 | bytes 24117248 | tf_op jit(solution)/shard_map/stack | solution.py:27
  207.9 1.0 copy-done
  208.9 3.9 select_bitcast_fusion
  212.8 17.6 %pad_maximum_fusion = bf16[3,2,8,512,512]{4,3,2,1,0:T(8,128)(2,1)} fusion(bf16[1,2,8,512,512]{4,3,2,1,0:T(8,128)(2,1)} %select_bitcast_fusion, bf16[1,2,8,512,512]{4,3,2,1,0:T(8,128)(2,1)} %bitcast.49, bf16[1,2,8,512,512]{4,3,2,1,0:T(8,128)(2,1)} %select_bitcast_fusion.1), kind=kLoop, calls=%fused_computation | loop fusion | flops 25165824 | bytes 50331648 | tf_op jit(solution)/shard_map/stack | solution.py:27
  230.4 11.3 %dynamic-slice_bitcast_fusion = (bf16[2,8,512,512]{3,2,1,0:T(8,128)(2,1)}, bf16[2,8,512,512]{3,2,1,0:T(8,128)(2,1)}) fusion(bf16[3,2,8,512,512]{4,3,2,1,0:T(8,128)(2,1)} %pad_maximum_fusion, s32[]{:T(128)S(6)} %select_n.30, s32[]{:T(128)S(6)} %select_n.29), kind=kLoop, calls=%fused_computation.11 | loop fusion | bytes 33554440 | tf_op jit(solution)/shard_map/jit(dynamic_index_in_dim)/squeeze | solution.py:30
  241.7 15.7 %fusion.4 = f32[8,2,512,512]{3,2,1,0:T(8,128)} fusion(bf16[2,8,512,512]{3,2,1,0:T(8,128)(2,1)} %get-tuple-element.6, bf16[2,8,512,512]{3,2,1,0:T(8,128)(2,1)} %param.7, bf16[2,8,512,512]{3,2,1,0:T(8,128)(2,1)} %param.6), kind=kOutput, calls=%fused_computation.4 | convolution fusion | flops 8594128896 | bytes 33554432 | tf_op jit(solution)/shard_map/ksac,scd->ksad/dot_general | solution.py:38
  257.4 24.1 %add_bitcast_fusion = f32[2,8,512,512]{3,2,0,1:T(8,128)} fusion(f32[8,2,512,512]{3,2,1,0:T(8,128)} %fusion.4, bf16[2,8,512,512]{3,2,1,0:T(8,128)(2,1)} %get-tuple-element.5, bf16[2,8,512,512]{3,2,1,0:T(8,128)(2,1)} %param.7, bf16[2,8,512,512]{3,2,1,0:T(8,128)(2,1)} %param.6), kind=kOutput, calls=%fused_computation.1 | convolution fusion | flops 8598323200 | bytes 50331648 | tf_op jit(solution)/shard_map/ksac,scd->ksad/dot_general | solution.py:38
  281.5 0.0 copy-start.1
  281.5 0.0 reduce-scatter.2.cloned.1.call-update
  281.5 0.6 copy-done.1
  282.1 0.1 broadcast_compare_fusion
  282.2 0.1 iota_compare_fusion
  282.3 0.3 broadcast_and_fusion
  282.6 284.4 %reduce-scatter.2.cloned.1.call-done = f32[2,8,128,512]{3,2,0,1:T(8,128)} async-done(((f32[2,8,512,512]{3,2,0,1:T(8,128)}), f32[2,8,128,512]{3,2,0,1:T(8,128)}) %reduce-scatter.2.cloned.1.call-update) | async-done | bytes 4194320 | tf_op jit(solution)/shard_map/reduce_scatter | solution.py:44
  567.0 2.9 select_convert_fusion
  569.9 1.5 copy.6
  (1 shorter events, 0.0 us)
Async XLA Ops:
  6.5 560.5 %reduce-scatter.2.cloned.1.call-start = ((), (), s32[]{:S(2)}) async-start(), calls=%async_computation.1 | async-start | bytes 20971520 | tf_op jit(solution)/shard_map/reduce_scatter | solution.py:44
  6.5 183.5 %collective-permute-start = (bf16[2,8,512,512]{3,2,1,0:T(8,128)(2,1)}, bf16[2,8,512,512]{3,2,1,0:T(8,128)(2,1)}, u32[]{:S(2)}, u32[]{:S(2)}) collective-permute-start(bf16[2,8,512,512]{3,2,1,0:T(8,128)(2,1)} %param.5), channel_id=1, source_target_pairs={{1,0},{2,1},{3,2},{4,3},{5,4},{6,5},{7,6},{0,7},{9,8},{10,9},{11,1... | collective-permute-start | bytes 25165832 | tf_op jit(solution)/shard_map/ppermute | solution.py:10
  9.9 183.8 %collective-permute-start.1 = (bf16[2,8,512,512]{3,2,1,0:T(8,128)(2,1)}, bf16[2,8,512,512]{3,2,1,0:T(8,128)(2,1)}, u32[]{:S(2)}, u32[]{:S(2)}) collective-permute-start(bf16[2,8,512,512]{3,2,1,0:T(8,128)(2,1)} %param.5), channel_id=1, source_target_pairs={{7,0},{0,1},{1,2},{2,3},{3,4},{4,5},{5,6},{6,7},{15,8},{8,9},{9,10... | collective-permute-start | bytes 25165832 | tf_op jit(solution)/shard_map/ppermute | solution.py:10
  200.3 8.6 %copy-start = (bf16[2,7,512,512]{3,2,1,0:T(8,128)(2,1)S(1)}, bf16[2,7,512,512]{3,2,1,0:T(8,128)(2,1)}, u32[]{:S(2)}) copy-start(bf16[2,7,512,512]{3,2,1,0:T(8,128)(2,1)} %slice.33) | copy-start | bytes 22020100
  281.5 0.7 copy-start.1
Sparse Core Ops, SparseCore 0:
  281.6 285.3 reduce-scatter.1
where the time goes:
time: 579 us; the launch traced here: 578 us
  waiting for transfers between devices  461 us (80%)
  matrix products  39.8 us (7%)
  other arithmetic  32.4 us (6%)
  local copies, waits for them, and re-layouts  25.9 us (4%)
  between operations  15.9 us (3%)
    reduce_scatter x1, waiting for transfers between devices, body(): lax.psum_scatter(accumulated, 'mpo', scatter_dimension=2, tiled=True)  284 us
    ppermute x2, waiting for transfers between devices, shifted(): return lax.ppermute(block, axis, route)  176 us
    dot_general x2, matrix products, body(): jnp.einsum('ksac,scd->ksad', left_parts[mpo_row], right_env[mpo_row], pre...  39.8 us
    another operation x3, other arithmetic, body(): variants = jnp.stack([from_upper, wavefunction, from_lower])  29.1 us
  transfers between devices with their start and end apart: 3, of which 2 were waited for; matrix products, arithmetic and copies ran while one was open for 1% of the time, Pallas kernels for 0%

commit v1 on v0

v1 whole, which is shorter than its diff:
```python
import functools

import jax
import jax.numpy as jnp
from jax import lax
from jax.experimental import pallas as pl
from jax.experimental.pallas import tpu as pltpu
from jax.sharding import PartitionSpec as P

GROUPS = 4


def apply_kernel(flags, dims, own, lower, upper, left, right, out, *, first_slot, group):
    step = pl.program_id(0)
    slot = first_slot + step
    vectors, size = own.shape[0], own.shape[2]
    chunks, rows = out.shape[0], out.shape[3]
    limit = dims[slot]
    sources = []
    for row in range(left.shape[0]):
        shift = flags[row]
        live = jnp.logical_not(
            jnp.logical_or(
                jnp.logical_and(jnp.logical_and(shift > 0, flags[left.shape[0]] == 1), slot == 0),
                jnp.logical_and(
                    jnp.logical_and(shift < 0, flags[left.shape[0] + 1] == 1), slot == group - 1
                ),
            )
        )
        sources.append((shift, live))
    for k in range(vectors):
        total = jnp.zeros((size, size), jnp.float32)
        for row, (shift, live) in enumerate(sources):
            chosen = jnp.where(
                shift > 0, lower[k, 0], jnp.where(shift < 0, upper[k, 0], own[k, 0])
            )
            chosen = jnp.where(live, chosen, jnp.zeros_like(chosen))
            part = jnp.dot(left[row, 0], chosen, preferred_element_type=jnp.float32)
            total += jnp.dot(
                part.astype(jnp.bfloat16), right[row, 0], preferred_element_type=jnp.float32
            )
        row_index = lax.broadcasted_iota(jnp.int32, (size, size), 0)
        col_index = lax.broadcasted_iota(jnp.int32, (size, size), 1)
        inside = jnp.logical_and(row_index < limit, col_index < limit)
        kept = jnp.where(inside, total, jnp.zeros_like(total)).astype(out.dtype)
        for chunk in range(chunks):
            out[chunk, k, 0] = kept[chunk * rows : (chunk + 1) * rows]


def apply_rows(flags, dims, own, lower, upper, left, right, first_slot, chunks):
    vectors, group, size, _ = lower.shape
    rows, slots = left.shape[0], left.shape[1]
    own_spec = pl.BlockSpec((vectors, 1, size, size), lambda i, *_: (0, first_slot + i, 0, 0))
    moved_spec = pl.BlockSpec((vectors, 1, size, size), lambda i, *_: (0, i, 0, 0))
    env_spec = pl.BlockSpec((rows, 1, size, size), lambda i, *_: (0, first_slot + i, 0, 0))
    return pl.pallas_call(
        functools.partial(apply_kernel, first_slot=first_slot, group=slots),
        grid_spec=pltpu.PrefetchScalarGridSpec(
            num_scalar_prefetch=2,
            grid=(group,),
            in_specs=[own_spec, moved_spec, moved_spec, env_spec, env_spec],
            out_specs=pl.BlockSpec(
                (chunks, vectors, 1, size // chunks, size), lambda i, *_: (0, 0, i, 0, 0)
            ),
        ),
        out_shape=jax.ShapeDtypeStruct(
            (chunks, vectors, group, size // chunks, size), jnp.bfloat16
        ),
        compiler_params=pltpu.CompilerParams(vmem_limit_bytes=40 * 1024 * 1024),
        cost_estimate=pl.CostEstimate(
            flops=group * vectors * rows * 4 * size**3,
            bytes_accessed=group * size * size * 2 * (4 * vectors + 2 * rows),
            transcendentals=0,
        ),
    )(flags, dims, own, lower, upper, left, right)


def body(wavefunction, left_env, right_env, block_dims, mpo_shift):
    sec_count = lax.axis_size("sec")
    sec_index = lax.axis_index("sec")
    chunks = lax.axis_size("mpo")
    slots = wavefunction.shape[1]
    is_first = (sec_index == 0).astype(jnp.int32)
    is_last = (sec_index == sec_count - 1).astype(jnp.int32)
    flags = jnp.concatenate([mpo_shift, is_first[None], is_last[None]])
    upward = [(i, (i + 1) % sec_count) for i in range(sec_count)]
    downward = [(i, (i - 1) % sec_count) for i in range(sec_count)]

    def picked(first, count, offset):
        parts = []
        for slot in range(first, first + count):
            at = jnp.clip(slot + offset, 0, slots - 1)
            parts.append(lax.dynamic_slice_in_dim(wavefunction, at, 1, 1))
        return jnp.concatenate(parts, axis=1)

    count = max(slots // GROUPS, 1)
    pieces, arrived = [], []
    for first in range(0, slots, count):
        to_upper = picked(first, count, -is_last)
        to_lower = picked(first, count, is_first)
        if len(arrived) >= 2:
            to_upper, to_lower, _ = lax.optimization_barrier((to_upper, to_lower, arrived[-2]))
        from_lower = lax.ppermute(to_upper, "sec", upward)
        from_upper = lax.ppermute(to_lower, "sec", downward)
        arrived.append((from_lower, from_upper))
        partial = apply_rows(
            flags,
            block_dims,
            wavefunction,
            from_lower,
            from_upper,
            left_env,
            right_env,
            first,
            chunks,
        )
        pieces.append(lax.psum_scatter(partial, "mpo", scatter_dimension=0))
    return jnp.concatenate(pieces, axis=1)


def solution(mesh):
    placed = (
        P(None, "sec", None, None),
        P("mpo", "sec", None, None),
        P("mpo", "sec", None, None),
        P("sec"),
        P("mpo"),
    )
    return jax.shard_map(
        body, mesh=mesh, in_specs=placed, out_specs=P(None, "sec", "mpo", None), check_vma=False
    )
```

time: 579 us -> 306 us (0.53)
  waiting for transfers between devices: 461 us -> 227 us
  matrix products: 39.8 us -> 0 us
  Pallas kernels: 0 us -> 33.4 us
  other arithmetic: 32.4 us -> 8.35 us
  local copies, waits for them, and re-layouts: 25.9 us -> 12.3 us
  starting transfers between devices: 3.34 us -> 11.5 us
    reduce_scatter x1 -> x4, waiting for transfers between devices: 284 us -> 44.4 us  [body(): pieces.append(lax.psum_scatter(partial, 'mpo', scatter_dimension=0))]
    dot_general x2 -> x0, matrix products: 39.8 us -> none  [body(): jnp.einsum('ksac,scd->ksad', left_parts[mpo_row], right_env[mpo_row], pre...]
    pallas_call x0 -> x4, Pallas kernels: none -> 33.4 us  [apply_rows(): pl.pallas_call(functools.partial(apply_kernel, first_slot=first_slot, gro...]
    another operation x3 -> x0, other arithmetic: 29.1 us -> none  [body(): variants = jnp.stack([from_upper, wavefunction, from_lower])]
    slice x3 -> x0, local copies, waits for them, and re-layouts: 11.5 us -> none  [the longest x1 6.57 us: body(): lower_raw[:, :-1]]
    squeeze x1 -> x0, local copies, waits for them, and re-layouts: 11.3 us -> none  [body(): lax.dynamic_index_in_dim(variants, mpo_shift[mpo_row] + 1, 0, keepdims=Fa...]
    dynamic_slice x0 -> x1, local copies, waits for them, and re-layouts: none -> 9.41 us  [picked(): parts.append(lax.dynamic_slice_in_dim(wavefunction, at, 1, 1))]
    concatenate x0 -> x8, other arithmetic: none -> 8.35 us  [the longest x6 5.17 us: picked(): return jnp.concatenate(parts, axis=1)]
  transfers between devices with their start and end apart: 3 -> 12, of which waited for: 2 -> 6; matrix products, arithmetic and copies ran while one was open for 1% -> 2% of each run, Pallas kernels for 0% -> 8%
where the time goes in v1:
time: 306 us; the launch traced here: 305 us
  waiting for transfers between devices  227 us (74%)
  Pallas kernels  33.4 us (11%)
  between operations  13.2 us (4%)
  local copies, waits for them, and re-layouts  12.3 us (4%)
  starting transfers between devices  11.5 us (4%)
  other arithmetic  8.35 us (3%)
    ppermute x4, waiting for transfers between devices, body(): from_lower = lax.ppermute(to_upper, 'sec', upward)  179 us
    reduce_scatter x4, waiting for transfers between devices, body(): pieces.append(lax.psum_scatter(partial, 'mpo', scatter_dimension=0))  44.4 us
    pallas_call x4, Pallas kernels, apply_rows(): pl.pallas_call(functools.partial(apply_kernel, first_slot=first_slot, gro...  33.4 us
    dynamic_slice x1, local copies, waits for them, and re-layouts, picked(): parts.append(lax.dynamic_slice_in_dim(wavefunction, at, 1, 1))  9.41 us
    ppermute x4, starting transfers between devices, body(): from_upper = lax.ppermute(to_lower, 'sec', downward)  6.93 us
  transfers between devices with their start and end apart: 12, of which 6 were waited for; matrix products, arithmetic and copies ran while one was open for 2% of the time, Pallas kernels for 8%

profile of v1, /device:TPU:0, one launch (start us, length us, event | category | flops | bytes accessed | tf_op | source)
XLA Modules:
  0.0 305.4 jit_solution(16014597333274263307)
XLA Ops:
  6.5 0.0 reduce-scatter.7.cloned.1.call-start
  6.5 9.4 %constant_dynamic-slice_fusion.13 = (bf16[2,1,512,512]{3,2,1,0:T(8,128)(2,1)S(1)}, bf16[2,1,512,512]{3,2,1,0:T(8,128)(2,1)}, bf16[2,1,512,512]{3,2,1,0:T(8,128)(...) fusion(bf16[2,8,512,512]{3,2,1,0:T(8,128)(2,1)} %own.7, ...), kind=kLoop, calls=%fused_computation.22 | loop fusion | bytes 33554496 | tf_op jit(solution)/shard_map/dynamic_slice | solution.py:93
  16.0 0.2 pad_maximum_fusion.2
  16.2 0.5 collective-permute-start.2
  16.7 0.0 copy-start.7
  16.7 0.0 copy-start
  16.7 0.2 pad_maximum_fusion.3
  16.9 2.5 collective-permute-start.3
  19.4 0.0 copy-done.7
  19.4 0.1 pad_add_fusion.flags
  19.5 42.5 %collective-permute-done.2.lower = bf16[2,2,512,512]{3,2,1,0:T(8,128)(2,1)S(1)} collective-permute-done((bf16[2,2,512,512]{3,2,1,0:T(8,128)(2,1)S(1)}, bf16[2,2,512,512]{3,2,1,0:T(8,128)(2,1)S(1)}, u32[]{:S(2)}, u32[]{:S(2)}) %collective-permute-start.2) | collective-permute-done | bytes 2097184 | tf_op jit(solution)/shard_map/ppermute | solution.py:103
  62.0 2.7 collective-permute-done.3.upper
  64.6 0.0 copy-done
  64.6 8.4 %shard_map.56 = bf16[4,2,2,128,512]{4,3,2,1,0:T(8,128)(2,1)} custom-call(s32[4]{0:T(128)S(1)} %pad_add_fusion.flags, s32[8]{0:T(128)S(1)} %copy-done, bf16[2,8,512,512]{3,2,1,0:T(8,128)(2,1)} %own.7, bf16[2,2,512,512]{3,2,1,0:T(8,128)(2,1)S(1)} %collective-permute-done.2.lower, bf16[2,2,512,512]{3,2,1,0:T(8,128)(2,1)S(1)} %collective-permute-done.3.upper, ...), custom_call_target="tpu_custom_call" | custom-call | flops 4294967296 | bytes 12582912 | tf_op jit(solution)/shard_map/pallas_call | solution.py:56
  73.0 0.0 reduce-scatter.7.cloned.1.call-update
  73.0 0.0 reduce-scatter.5.cloned.1.call-start
  73.1 1.4 pad_maximum_fusion
  74.5 1.8 collective-permute-start
  76.3 0.2 pad_maximum_fusion.1
  76.5 1.1 collective-permute-start.1
  77.6 45.0 %collective-permute-done.lower = bf16[2,2,512,512]{3,2,1,0:T(8,128)(2,1)S(1)} collective-permute-done((bf16[2,2,512,512]{3,2,1,0:T(8,128)(2,1)S(1)}, bf16[2,2,512,512]{3,2,1,0:T(8,128)(2,1)S(1)}, u32[]{:S(2)}, u32[]{:S(2)}) %collective-permute-start) | collective-permute-done | bytes 2097184 | tf_op jit(solution)/shard_map/ppermute | solution.py:103
  122.6 0.0 collective-permute-done.1.upper
  122.6 0.0 copy-start.6
  122.6 8.3 %shard_map.55 = bf16[4,2,2,128,512]{4,3,2,1,0:T(8,128)(2,1)} custom-call(s32[4]{0:T(128)S(1)} %pad_add_fusion.flags, s32[8]{0:T(128)S(1)} %copy-done, bf16[2,8,512,512]{3,2,1,0:T(8,128)(2,1)} %own.7, bf16[2,2,512,512]{3,2,1,0:T(8,128)(2,1)S(1)} %collective-permute-done.lower, bf16[2,2,512,512]{3,2,1,0:T(8,128)(2,1)S(1)} %collective-permute-done.1.upper, ...), custom_call_target="tpu_custom_call" | custom-call | flops 4294967296 | bytes 12582912 | tf_op jit(solution)/shard_map/pallas_call | solution.py:56
  131.0 0.0 copy-start.4
  131.0 0.0 copy-start.5
  131.0 0.0 reduce-scatter.5.cloned.1.call-update
  131.0 0.0 reduce-scatter.11.cloned.1.call-start
  131.0 0.0 copy-done.6
  131.0 1.1 copy-done.4
  132.2 0.3 copy-done.5
  132.5 1.6 pad_maximum_fusion.6
  134.1 1.5 collective-permute-start.6
  135.6 1.2 collective-permute-start.7
  136.8 45.9 %collective-permute-done.6.lower = bf16[2,2,512,512]{3,2,1,0:T(8,128)(2,1)S(1)} collective-permute-done((bf16[2,2,512,512]{3,2,1,0:T(8,128)(2,1)S(1)}, bf16[2,2,512,512]{3,2,1,0:T(8,128)(2,1)S(1)}, u32[]{:S(2)}, u32[]{:S(2)}) %collective-permute-start.6) | collective-permute-done | bytes 2097184 | tf_op jit(solution)/shard_map/ppermute | solution.py:103
  182.7 0.0 collective-permute-done.7.upper
  182.7 0.0 copy-start.3
  182.7 8.4 %shard_map.58 = bf16[4,2,2,128,512]{4,3,2,1,0:T(8,128)(2,1)} custom-call(s32[4]{0:T(128)S(1)} %pad_add_fusion.flags, s32[8]{0:T(128)S(1)} %copy-done, bf16[2,8,512,512]{3,2,1,0:T(8,128)(2,1)} %own.7, bf16[2,2,512,512]{3,2,1,0:T(8,128)(2,1)S(1)} %collective-permute-done.6.lower, bf16[2,2,512,512]{3,2,1,0:T(8,128)(2,1)S(1)} %collective-permute-done.7.upper, ...), custom_call_target="tpu_custom_call" | custom-call | flops 4294967296 | bytes 12582912 | tf_op jit(solution)/shard_map/pallas_call | solution.py:56
  191.0 0.0 copy-start.1
  191.0 0.0 copy-start.2
  191.0 0.0 reduce-scatter.11.cloned.1.call-update
  191.0 0.0 reduce-scatter.9.cloned.1.call-start
  191.1 0.0 copy-done.3
  191.1 1.1 copy-done.1
  192.2 0.3 copy-done.2
  192.6 1.6 pad_maximum_fusion.4
  194.1 0.6 collective-permute-start.4
  194.8 2.1 collective-permute-start.5
  196.8 46.1 %collective-permute-done.4.lower = bf16[2,2,512,512]{3,2,1,0:T(8,128)(2,1)S(1)} collective-permute-done((bf16[2,2,512,512]{3,2,1,0:T(8,128)(2,1)S(1)}, bf16[2,2,512,512]{3,2,1,0:T(8,128)(2,1)S(1)}, u32[]{:S(2)}, u32[]{:S(2)}) %collective-permute-start.4) | collective-permute-done | bytes 2097184 | tf_op jit(solution)/shard_map/ppermute | solution.py:103
  243.0 0.0 collective-permute-done.5.upper
  243.0 8.4 %shard_map.57 = bf16[4,2,2,128,512]{4,3,2,1,0:T(8,128)(2,1)} custom-call(s32[4]{0:T(128)S(1)} %pad_add_fusion.flags, s32[8]{0:T(128)S(1)} %copy-done, bf16[2,8,512,512]{3,2,1,0:T(8,128)(2,1)} %own.7, bf16[2,2,512,512]{3,2,1,0:T(8,128)(2,1)S(1)} %collective-permute-done.4.lower, bf16[2,2,512,512]{3,2,1,0:T(8,128)(2,1)S(1)} %collective-permute-done.5.upper, ...), custom_call_target="tpu_custom_call" | custom-call | flops 4294967296 | bytes 12582912 | tf_op jit(solution)/shard_map/pallas_call | solution.py:56
  251.3 0.0 reduce-scatter.9.cloned.1.call-update
  251.4 0.0 reduce-scatter.7.cloned.1.call-done
  251.4 0.0 reduce-scatter.5.cloned.1.call-done
  251.4 0.0 reduce-scatter.11.cloned.1.call-done
  251.4 44.3 %reduce-scatter.9.cloned.1.call-done = bf16[1,2,2,128,512]{4,3,2,1,0:T(8,128)(2,1)} async-done(((bf16[4,2,2,128,512]{4,3,2,1,0:T(8,128)(2,1)}), bf16[1,2,2,128,512]{4,3,2,1,0:T(8,128)(2,1)}) %reduce-scatter.9.cloned.1.call-update) | async-done | bytes 524304 | tf_op jit(solution)/shard_map/reduce_scatter | solution.py:117
  295.8 3.1 %pad_maximum_fusion.8 = bf16[2,8,128,512]{3,2,1,0:T(8,128)(2,1)} fusion(bf16[2,2,128,512]{3,2,1,0:T(8,128)(2,1)} %bitcast.8, bf16[2,2,128,512]{3,2,1,0:T(8,128)(2,1)} %bitcast.9, bf16[2,2,128,512]{3,2,1,0:T(8,128)(2,1)} %bitcast.6, bf16[2,2,128,512]{3,2,1,0:T(8,128)(2,1)} %bitcast.7), kind=kLoop, calls=%fused_computation.8 | loop fusion | flops 3145728 | bytes 4194304 | tf_op jit(solution)/shard_map/concatenate | solution.py:118
Async XLA Ops:
  6.5 244.8 %reduce-scatter.7.cloned.1.call-start = ((), (), s32[]{:S(2)}) async-start(), calls=%async_computation.5 | async-start | bytes 2621440 | tf_op jit(solution)/shard_map/reduce_scatter | solution.py:117
  16.2 45.8 %collective-permute-start.2 = (bf16[2,2,512,512]{3,2,1,0:T(8,128)(2,1)S(1)}, bf16[2,2,512,512]{3,2,1,0:T(8,128)(2,1)S(1)}, u32[]{:S(2)}, u32[]{:S(2)}) collective-permute-start(bf16[2,2,512,512]{3,2,1,0:T(8,128)(2,1)S(1)} %pad_maximum_fusion.2), channel_id=1, source_target_pairs={{0,1},{1,2},{2,3},{3,4},{4,5},{5,6},{6,7},{7,0},{8,9},{9,10},{10,1... | collective-permute-start | bytes 6291464 | tf_op jit(solution)/shard_map/ppermute | solution.py:103
  16.7 2.7 copy-start.7
  16.7 47.9 %copy-start = (s32[8]{0:T(128)S(1)}, s32[8]{0:T(128)}, u32[]{:S(2)}) copy-start(s32[8]{0:T(128)} %dims.7) | copy-start | bytes 100
  16.9 47.7 %collective-permute-start.3 = (bf16[2,2,512,512]{3,2,1,0:T(8,128)(2,1)S(1)}, bf16[2,2,512,512]{3,2,1,0:T(8,128)(2,1)S(1)}, u32[]{:S(2)}, u32[]{:S(2)}) collective-permute-start(bf16[2,2,512,512]{3,2,1,0:T(8,128)(2,1)S(1)} %pad_maximum_fusion.3), channel_id=1, source_target_pairs={{0,7},{1,0},{2,1},{3,2},{4,3},{5,4},{6,5},{7,6},{8,15},{9,8},{10,9... | collective-permute-start | bytes 6291464 | tf_op jit(solution)/shard_map/ppermute | solution.py:104
  73.0 178.4 %reduce-scatter.5.cloned.1.call-start = ((), (), s32[]{:S(2)}) async-start(), calls=%async_computation.4 | async-start | bytes 2621440 | tf_op jit(solution)/shard_map/reduce_scatter | solution.py:117
  74.5 48.1 %collective-permute-start = (bf16[2,2,512,512]{3,2,1,0:T(8,128)(2,1)S(1)}, bf16[2,2,512,512]{3,2,1,0:T(8,128)(2,1)S(1)}, u32[]{:S(2)}, u32[]{:S(2)}) collective-permute-start(bf16[2,2,512,512]{3,2,1,0:T(8,128)(2,1)S(1)} %pad_maximum_fusion), channel_id=1, source_target_pairs={{0,1},{1,2},{2,3},{3,4},{4,5},{5,6},{6,7},{7,0},{8,9},{9,10},{10,1... | collective-permute-start | bytes 6291464 | tf_op jit(solution)/shard_map/ppermute | solution.py:103
  76.5 46.1 %collective-permute-start.1 = (bf16[2,2,512,512]{3,2,1,0:T(8,128)(2,1)S(1)}, bf16[2,2,512,512]{3,2,1,0:T(8,128)(2,1)S(1)}, u32[]{:S(2)}, u32[]{:S(2)}) collective-permute-start(bf16[2,2,512,512]{3,2,1,0:T(8,128)(2,1)S(1)} %pad_maximum_fusion.1), channel_id=1, source_target_pairs={{0,7},{1,0},{2,1},{3,2},{4,3},{5,4},{6,5},{7,6},{8,15},{9,8},{10,9... | collective-permute-start | bytes 6291464 | tf_op jit(solution)/shard_map/ppermute | solution.py:104
  122.6 8.4 %copy-start.6 = (bf16[2,1,512,512]{3,2,1,0:T(8,128)(2,1)S(1)}, bf16[2,1,512,512]{3,2,1,0:T(8,128)(2,1)}, u32[]{:S(2)}) copy-start(bf16[2,1,512,512]{3,2,1,0:T(8,128)(2,1)} %get-tuple-element.16) | copy-start | bytes 3145732
  131.0 1.2 copy-start.4
  131.0 1.5 copy-start.5
  131.0 120.5 %reduce-scatter.11.cloned.1.call-start = ((), (), s32[]{:S(2)}) async-start(), calls=%async_computation.7 | async-start | bytes 2621440 | tf_op jit(solution)/shard_map/reduce_scatter | solution.py:117
  134.1 48.6 %collective-permute-start.6 = (bf16[2,2,512,512]{3,2,1,0:T(8,128)(2,1)S(1)}, bf16[2,2,512,512]{3,2,1,0:T(8,128)(2,1)S(1)}, u32[]{:S(2)}, u32[]{:S(2)}) collective-permute-start(bf16[2,2,512,512]{3,2,1,0:T(8,128)(2,1)S(1)} %get-tuple-element.11), channel_id=1, source_target_pairs={{0,1},{1,2},{2,3},{3,4},{4,5},{5,6},{6,7},{7,0},{8,9},{9,10},{10,1... | collective-permute-start | bytes 6291464 | tf_op jit(solution)/shard_map/ppermute | solution.py:103
  135.6 47.1 %collective-permute-start.7 = (bf16[2,2,512,512]{3,2,1,0:T(8,128)(2,1)S(1)}, bf16[2,2,512,512]{3,2,1,0:T(8,128)(2,1)S(1)}, u32[]{:S(2)}, u32[]{:S(2)}) collective-permute-start(bf16[2,2,512,512]{3,2,1,0:T(8,128)(2,1)S(1)} %get-tuple-element.12), channel_id=1, source_target_pairs={{0,7},{1,0},{2,1},{3,2},{4,3},{5,4},{6,5},{7,6},{8,15},{9,8},{10,9... | collective-permute-start | bytes 6291464 | tf_op jit(solution)/shard_map/ppermute | solution.py:104
  182.7 8.4 %copy-start.3 = (bf16[2,1,512,512]{3,2,1,0:T(8,128)(2,1)S(1)}, bf16[2,1,512,512]{3,2,1,0:T(8,128)(2,1)}, u32[]{:S(2)}) copy-start(bf16[2,1,512,512]{3,2,1,0:T(8,128)(2,1)} %get-tuple-element.19) | copy-start | bytes 3145732
  191.0 1.2 copy-start.1
  191.0 1.5 copy-start.2
  191.0 104.7 %reduce-scatter.9.cloned.1.call-start = ((), (), s32[]{:S(2)}) async-start(), calls=%async_computation.6 | async-start | bytes 2621440 | tf_op jit(solution)/shard_map/reduce_scatter | solution.py:117
  194.1 48.8 %collective-permute-start.4 = (bf16[2,2,512,512]{3,2,1,0:T(8,128)(2,1)S(1)}, bf16[2,2,512,512]{3,2,1,0:T(8,128)(2,1)S(1)}, u32[]{:S(2)}, u32[]{:S(2)}) collective-permute-start(bf16[2,2,512,512]{3,2,1,0:T(8,128)(2,1)S(1)} %get-tuple-element.9), channel_id=1, source_target_pairs={{0,1},{1,2},{2,3},{3,4},{4,5},{5,6},{6,7},{7,0},{8,9},{9,10},{10,1... | collective-permute-start | bytes 6291464 | tf_op jit(solution)/shard_map/ppermute | solution.py:103
  194.8 48.2 %collective-permute-start.5 = (bf16[2,2,512,512]{3,2,1,0:T(8,128)(2,1)S(1)}, bf16[2,2,512,512]{3,2,1,0:T(8,128)(2,1)S(1)}, u32[]{:S(2)}, u32[]{:S(2)}) collective-permute-start(bf16[2,2,512,512]{3,2,1,0:T(8,128)(2,1)S(1)} %get-tuple-element.10), channel_id=1, source_target_pairs={{0,7},{1,0},{2,1},{3,2},{4,3},{5,4},{6,5},{7,6},{8,15},{9,8},{10,9... | collective-permute-start | bytes 6291464 | tf_op jit(solution)/shard_map/ppermute | solution.py:104
Sparse Core Ops, SparseCore 0:
  73.2 45.5 reduce-scatter.6
  131.1 45.3 reduce-scatter.4
  191.2 45.2 reduce-scatter.10
  251.5 44.2 reduce-scatter.8

commit v2 on v1

v2 whole, which is shorter than its diff:
```python
import functools

import jax
import jax.numpy as jnp
from jax import lax
from jax.experimental import pallas as pl
from jax.experimental.pallas import tpu as pltpu
from jax.sharding import PartitionSpec as P

COST = 20
PLAN = 'A1s0 D2r1 D2r0 D2r0 D1s0'


def apply_kernel(flags, dims, *refs, first_slot, slots):
    sources, (left, right, out) = refs[:-3], refs[-3:]
    step = pl.program_id(0)
    slot = first_slot + step
    rows = left.shape[0]
    vectors, size = sources[0].shape[0], sources[0].shape[2]
    chunks, slab = out.shape[0], out.shape[3]
    limit = dims[slot]
    row_index = lax.broadcasted_iota(jnp.int32, (size, size), 0)
    col_index = lax.broadcasted_iota(jnp.int32, (size, size), 1)
    inside = jnp.logical_and(row_index < limit, col_index < limit)
    for k in range(vectors):
        total = jnp.zeros((size, size), jnp.float32)
        for row in range(rows):
            pick, edge = flags[row], flags[rows + row]
            live = jnp.logical_not(
                jnp.logical_or(
                    jnp.logical_and(edge > 0, slot == 0),
                    jnp.logical_and(edge < 0, slot == slots - 1),
                )
            )
            chosen = sources[0][k, 0]
            for i in range(1, len(sources)):
                chosen = jnp.where(pick == i, sources[i][k, 0], chosen)
            chosen = jnp.where(live, chosen, jnp.zeros_like(chosen))
            part = jnp.dot(left[row, 0], chosen, preferred_element_type=jnp.float32)
            total += jnp.dot(
                part.astype(jnp.bfloat16), right[row, 0], preferred_element_type=jnp.float32
            )
        kept = jnp.where(inside, total, jnp.zeros_like(total)).astype(out.dtype)
        for chunk in range(chunks):
            out[chunk, k, 0] = kept[chunk * slab : (chunk + 1) * slab]


def apply_rows(flags, dims, own, moved, left, right, first_slot, chunks):
    vectors, group, size, _ = moved[0].shape
    rows, slots = left.shape[0], left.shape[1]
    own_spec = pl.BlockSpec((vectors, 1, size, size), lambda i, *_: (0, first_slot + i, 0, 0))
    moved_spec = pl.BlockSpec((vectors, 1, size, size), lambda i, *_: (0, i, 0, 0))
    env_spec = pl.BlockSpec((rows, 1, size, size), lambda i, *_: (0, first_slot + i, 0, 0))
    return pl.pallas_call(
        functools.partial(apply_kernel, first_slot=first_slot, slots=slots),
        grid_spec=pltpu.PrefetchScalarGridSpec(
            num_scalar_prefetch=2,
            grid=(group,),
            in_specs=[own_spec] + [moved_spec] * len(moved) + [env_spec, env_spec],
            out_specs=pl.BlockSpec(
                (chunks, vectors, 1, size // chunks, size), lambda i, *_: (0, 0, i, 0, 0)
            ),
        ),
        out_shape=jax.ShapeDtypeStruct(
            (chunks, vectors, group, size // chunks, size), jnp.bfloat16
        ),
        compiler_params=pltpu.CompilerParams(vmem_limit_bytes=40 * 1024 * 1024),
        cost_estimate=pl.CostEstimate(
            flops=COST * group * vectors * rows * 4 * size**3,
            bytes_accessed=COST * group * size * size * 2 * (4 * vectors + 2 * rows),
            transcendentals=0,
        ),
    )(flags, dims, own, *moved, left, right)


def body(wavefunction, left_env, right_env, block_dims, mpo_shift):
    sec_count, planes = lax.axis_size("sec"), lax.axis_size("mpo")
    sec_index, plane = lax.axis_index("sec"), lax.axis_index("mpo")
    slots = wavefunction.shape[1]
    is_first = (sec_index == 0).astype(jnp.int32)
    is_last = (sec_index == sec_count - 1).astype(jnp.int32)
    odd = plane % 2
    forwards = sec_index % 2 == odd

    edge = jnp.where(mpo_shift > 0, is_first, jnp.where(mpo_shift < 0, -is_last, 0))
    direct_pick = jnp.where(mpo_shift > 0, 1, jnp.where(mpo_shift < 0, 2, 0))
    shared_pick = jnp.where(
        mpo_shift == 0, 0, jnp.where((mpo_shift > 0) == (odd == 0), 1, 2)
    )
    direct_flags = jnp.concatenate([direct_pick, edge]).astype(jnp.int32)
    shared_flags = jnp.concatenate([shared_pick, edge]).astype(jnp.int32)

    upward = [(i, (i + 1) % sec_count) for i in range(sec_count)]
    downward = [(i, (i - 1) % sec_count) for i in range(sec_count)]
    both = [
        (m * sec_count + i, m * sec_count + j)
        for m in range(planes)
        for i, j in (upward if m % 2 == 0 else downward)
    ]
    passed = [
        (m * sec_count + i, (m ^ 1) * sec_count + i if i % 2 == m % 2 else m * sec_count + (i ^ 1))
        for m in range(planes)
        for i in range(sec_count)
    ]
    can_share = planes % 2 == 0 and sec_count % 2 == 0

    def picked(source, first, count, offset):
        parts = []
        for slot in range(first, first + count):
            at = jnp.clip(slot + offset, 0, slots - 1)
            parts.append(lax.dynamic_slice_in_dim(source, at, 1, 1))
        return jnp.concatenate(parts, axis=1)

    def sent_sum(partial):
        total = lax.dynamic_index_in_dim(partial, plane, 0, keepdims=False).astype(jnp.float32)
        for distance in range(1, planes):
            target = (plane + distance) % planes
            came = lax.ppermute(
                lax.dynamic_index_in_dim(partial, target, 0, keepdims=False),
                "mpo",
                [(m, (m + distance) % planes) for m in range(planes)],
            )
            total += came.astype(jnp.float32)
        return total.astype(jnp.bfloat16)

    pieces, partials, arrived = [], [], []
    first, count = 0, 0
    for fetch, width, reduce, lag in PLAN.split():
        first, count = first + count, int(width)
        source = wavefunction
        if int(lag) and len(arrived) >= int(lag):
            source, _ = lax.optimization_barrier((source, arrived[-int(lag)]))
        elif len(partials) >= 2:
            source, _ = lax.optimization_barrier((source, partials[-2]))
        if fetch == "A" and can_share:
            to_upper = picked(source, first, count, -is_last)
            to_lower = picked(source, first, count, is_first)
            fetched = lax.ppermute(
                jnp.where(odd == 0, to_upper, to_lower), ("mpo", "sec"), both
            )
            arrived.append(fetched)
            own_side = jnp.where(odd == 0, to_lower, to_upper)
            moved = (
                fetched,
                lax.ppermute(jnp.where(forwards, fetched, own_side), ("mpo", "sec"), passed),
            )
            flags = shared_flags
        else:
            from_lower = lax.ppermute(picked(source, first, count, -is_last), "sec", upward)
            from_upper = lax.ppermute(picked(source, first, count, is_first), "sec", downward)
            moved = (from_lower, from_upper)
            arrived.append(moved)
            flags = direct_flags
        partial = apply_rows(
            flags, block_dims, wavefunction, moved, left_env, right_env, first, planes
        )
        partials.append(partial)
        if reduce == "r":
            pieces.append(lax.psum_scatter(partial, "mpo", scatter_dimension=0))
        else:
            pieces.append(sent_sum(partial))
    return jnp.concatenate(pieces, axis=1)


def solution(mesh):
    placed = (
        P(None, "sec", None, None),
        P("mpo", "sec", None, None),
        P("mpo", "sec", None, None),
        P("sec"),
        P("mpo"),
    )
    return jax.shard_map(
        body, mesh=mesh, in_specs=placed, out_specs=P(None, "sec", "mpo", None), check_vma=False
    )
```

time: 306 us -> 253 us (0.83)
  waiting for transfers between devices: 227 us -> 151 us
  starting transfers between devices: 11.5 us -> 23.1 us
  local copies, waits for them, and re-layouts: 12.3 us -> 17.3 us
  other arithmetic: 8.35 us -> 12.5 us
    ppermute x8 -> x16, waiting for transfers between devices: 182 us -> 119 us  [the longest x4 74.7 us: body(): lax.ppermute(picked(source, first, count, -is_last), 'sec', upward)]
    reduce_scatter x4 -> x3, waiting for transfers between devices: 44.4 us -> 32.6 us  [body(): pieces.append(lax.psum_scatter(partial, 'mpo', scatter_dimension=0))]
    ppermute x8 -> x16, starting transfers between devices: 11.4 us -> 23 us  [the longest x4 11.3 us: body(): lax.ppermute(picked(source, first, count, is_first), 'sec', downward)]
    unnamed x16 -> x13, local copies, waits for them, and re-layouts: 2.93 us -> 9.07 us
    select_n x0 -> x3, other arithmetic: none -> 4.31 us  [the longest x1 2.65 us: body(): jnp.where(forwards, fetched, own_side)]
    pallas_call x4 -> x5, Pallas kernels: 33.4 us -> 35.4 us  [apply_rows(): pl.pallas_call(functools.partial(apply_kernel, first_slot=first_slot, slo...]
    dynamic_slice x1 -> x4, local copies, waits for them, and re-layouts: 9.41 us -> 8.08 us  [picked(): parts.append(lax.dynamic_slice_in_dim(source, at, 1, 1))]
  transfers between devices with their start and end apart: 12 -> 19, of which waited for: 6 -> 13; matrix products, arithmetic and copies ran while one was open for 2% -> 8% of each run, Pallas kernels for 8% -> 14%
where the time goes in v2:
time: 253 us
  waiting for transfers between devices  151 us (60%)
  Pallas kernels  35.4 us (14%)
  starting transfers between devices  23.1 us (9%)
  local copies, waits for them, and re-layouts  17.3 us (7%)
  between operations  13.2 us (5%)
  other arithmetic  12.5 us (5%)
    ppermute x4, waiting for transfers between devices, body(): lax.ppermute(picked(source, first, count, -is_last), 'sec', upward)  74.7 us
    pallas_call x5, Pallas kernels, apply_rows(): pl.pallas_call(functools.partial(apply_kernel, first_slot=first_slot, slo...  35.4 us
    reduce_scatter x3, waiting for transfers between devices, body(): pieces.append(lax.psum_scatter(partial, 'mpo', scatter_dimension=0))  32.6 us
    ppermute x6, waiting for transfers between devices, sent_sum(): lax.ppermute(lax.dynamic_index_in_dim(partial, target, 0, keepdims=False)...  20 us
    ppermute x1, waiting for transfers between devices, body(): lax.ppermute(jnp.where(odd == 0, to_upper, to_lower), ('mpo', 'sec'), both)  15.4 us
    ppermute x4, starting transfers between devices, body(): lax.ppermute(picked(source, first, count, is_first), 'sec', downward)  11.3 us
    ppermute x6, starting transfers between devices, sent_sum(): lax.ppermute(lax.dynamic_index_in_dim(partial, target, 0, keepdims=False)...  9.74 us
    unnamed x13, local copies, waits for them, and re-layouts  9.07 us
  transfers between devices with their start and end apart: 19, of which 13 were waited for; matrix products, arithmetic and copies ran while one was open for 8% of the time, Pallas kernels for 14%

profile of v2, /device:TPU:0, one launch (start us, length us, event | category | flops | bytes accessed | tf_op | source)
XLA Modules:
  0.0 252.9 jit_solution(15724928624326055714)
XLA Ops:
  6.5 1.7 broadcast_select_fusion
  8.2 0.5 collective-permute-start
  8.7 15.4 %collective-permute-done.refs_1_ = bf16[2,1,512,512]{3,2,1,0:T(8,128)(2,1)S(1)} collective-permute-done((bf16[2,1,512,512]{3,2,1,0:T(8,128)(2,1)S(1)}, bf16[2,1,512,512]{3,2,1,0:T(8,128)(2,1)S(1)}, u32[]{:S(2)}, u32[]{:S(2)}) %collective-permute-start) | collective-permute-done | bytes 1048608 | tf_op jit(solution)/shard_map/ppermute | solution.py:138
  24.1 2.6 %select_select_fusion = bf16[2,1,512,512]{3,2,1,0:T(8,128)(2,1)} fusion(bf16[2,1,512,512]{3,2,1,0:T(8,128)(2,1)S(1)} %collective-permute-done.refs_1_, pred[]{:T(512)S(6)} %eq.38, pred[]{:T(512)S(6)} %eq.33, bf16[2,8,512,512]{3,2,1,0:T(8,128)(2,1)} %refs_0_.9, s32[]{:T(128)S(6)} %min.50, s32[]{:T(128)S(6)} %min.49), kind=kLoop, calls=%fused_computation.6 | loop fusion | flops 1048576 | bytes 4194314 | tf_op jit(solution)/shard_map/jit(_where)/select_n | solution.py:145
  26.7 1.4 collective-permute-start.1
  28.1 0.1 pad_add_fusion.1
  28.2 2.6 %constant_dynamic-slice_fusion.11 = (bf16[2,1,512,512]{3,2,1,0:T(8,128)(2,1)S(1)}, bf16[2,1,512,512]{3,2,1,0:T(8,128)(2,1)S(1)}, bf16[2,1,512,512]{3,2,1,0:T(8,128)(2,1)S(1)}, bf16[2,1,512,512]{3,2,1,0:T(8,128)(2,1)S(1)}) fusion(bf16[2,8,512,512]{3,2,1,0:T(8,128)(2,1)} %refs_0_.9, s32[]{:T(128)S(6)} %min.53, s32[]{:T(128)S(6)} %min.54, s32[]{:T(128)S(6)} %min.52, ...), kind=kLoop, calls=%fused_computation.39 | loop fusion | bytes 8388624 | tf_op jit(solution)/shard_map/dynamic_slice | solution.py:111
  30.8 0.0 slice-start.1
  30.8 0.2 pad_maximum_fusion
  31.0 0.1 collective-permute-start.5
  31.1 0.0 copy-start.1
  31.1 0.2 pad_maximum_fusion.1
  31.3 2.7 %collective-permute-start.6 = (bf16[2,2,512,512]{3,2,1,0:T(8,128)(2,1)S(1)}, bf16[2,2,512,512]{3,2,1,0:T(8,128)(2,1)S(1)}, u32[]{:S(2)}, u32[]{:S(2)}) collective-permute-start(bf16[2,2,512,512]{3,2,1,0:T(8,128)(2,1)S(1)} %pad_maximum_fusion.1), channel_id=1, source_target_pairs={{0,7},{1,0},{2,1},{3,2},{4,3},{5,4},{6,5},{7,6},{8,15},{9,8},{10,9... | collective-permute-start | bytes 6291464 | tf_op jit(solution)/shard_map/ppermute | solution.py:150
  34.0 6.8 %collective-permute-done.1.refs_2_ = bf16[2,1,512,512]{3,2,1,0:T(8,128)(2,1)S(1)} collective-permute-done((bf16[2,1,512,512]{3,2,1,0:T(8,128)(2,1)}, bf16[2,1,512,512]{3,2,1,0:T(8,128)(2,1)S(1)}, u32[]{:S(2)}, u32[]{:S(2)}) %collective-permute-start.1) | collective-permute-done | bytes 1048608 | tf_op jit(solution)/shard_map/ppermute | solution.py:145
  40.8 4.6 %shard_map.55 = bf16[4,2,1,128,512]{4,3,2,1,0:T(8,128)(2,1)S(1)} custom-call(s32[4]{0:T(128)S(1)} %get-tuple-element.34.flags, s32[8]{0:T(128)S(1)} %copy-done.1, bf16[2,8,512,512]{3,2,1,0:T(8,128)(2,1)S(1)} %bitcast.30, bf16[2,1,512,512]{3,2,1,0:T(8,128)(2,1)S(1)} %collective-permute-done.refs_1_, ...), custom_call_target="tpu_custom_call" | custom-call | flops 42949672960 | bytes 125829120 | tf_op jit(solution)/shard_map/pallas_call | solution.py:54
  45.4 0.1 dynamic-slice_bitcast_fusion.5
  45.4 4.5 %collective-permute-start.4 = (bf16[2,1,128,512]{3,2,1,0:T(8,128)(2,1)S(1)}, bf16[2,1,128,512]{3,2,1,0:T(8,128)(2,1)S(1)}, u32[]{:S(2)}, u32[]{:S(2)}) collective-permute-start(bf16[2,1,128,512]{3,2,1,0:T(8,128)(2,1)S(1)} %get-tuple-element.31), channel_id=1, source_target_pairs={{0,24},{8,0},{16,8},{24,16},{1,25},{9,1},{17,9},{25,17},{2,26},{10... | collective-permute-start | bytes 786440 | tf_op jit(solution)/shard_map/ppermute | solution.py:118
  49.9 0.0 collective-permute-start.3
  49.9 0.6 collective-permute-start.2
  50.5 0.3 constant_dynamic-slice_fusion.7
  50.8 1.5 pad_maximum_fusion.2
  52.3 1.5 pad_maximum_fusion.3
  53.8 2.9 %collective-permute-done.4 = bf16[2,1,128,512]{3,2,1,0:T(8,128)(2,1)S(1)} collective-permute-done((bf16[2,1,128,512]{3,2,1,0:T(8,128)(2,1)S(1)}, bf16[2,1,128,512]{3,2,1,0:T(8,128)(2,1)S(1)}, u32[]{:S(2)}, u32[]{:S(2)}) %collective-permute-start.4) | collective-permute-done | bytes 262176 | tf_op jit(solution)/shard_map/ppermute | solution.py:118
  56.7 0.0 collective-permute-start.7
  56.7 14.4 %collective-permute-done.3 = bf16[2,1,128,512]{3,2,1,0:T(8,128)(2,1)S(1)} collective-permute-done((bf16[2,1,128,512]{3,2,1,0:T(8,128)(2,1)S(1)}, bf16[2,1,128,512]{3,2,1,0:T(8,128)(2,1)S(1)}, u32[]{:S(2)}, u32[]{:S(2)}) %collective-permute-start.3) | collective-permute-done | bytes 262176 | tf_op jit(solution)/shard_map/ppermute | solution.py:118
  71.1 2.7 %collective-permute-start.8 = (bf16[2,2,512,512]{3,2,1,0:T(8,128)(2,1)}, bf16[2,2,512,512]{3,2,1,0:T(8,128)(2,1)}, u32[]{:S(2)}, u32[]{:S(2)}) collective-permute-start(bf16[2,2,512,512]{3,2,1,0:T(8,128)(2,1)} %pad_maximum_fusion.3), channel_id=1, source_target_pairs={{0,7},{1,0},{2,1},{3,2},{4,3},{5,4},{6,5},{7,6},{8,15},{9,8},{10,9... | collective-permute-start | bytes 6291464 | tf_op jit(solution)/shard_map/ppermute | solution.py:150
  73.8 0.0 collective-permute-done.2
  73.8 0.8 fusion.6
  74.6 4.8 %collective-permute-done.5.refs_1_ = bf16[2,2,512,512]{3,2,1,0:T(8,128)(2,1)S(1)} collective-permute-done((bf16[2,2,512,512]{3,2,1,0:T(8,128)(2,1)S(1)}, bf16[2,2,512,512]{3,2,1,0:T(8,128)(2,1)S(1)}, u32[]{:S(2)}, u32[]{:S(2)}) %collective-permute-start.5) | collective-permute-done | bytes 2097184 | tf_op jit(solution)/shard_map/ppermute | solution.py:149
  79.4 0.6 collective-permute-done.6.refs_2_
  80.1 8.5 %shard_map.56 = bf16[4,2,2,128,512]{4,3,2,1,0:T(8,128)(2,1)} custom-call(s32[4]{0:T(128)S(1)} %get-tuple-element.33.flags, s32[8]{0:T(128)S(1)} %copy-done.1, bf16[2,8,512,512]{3,2,1,0:T(8,128)(2,1)} %refs_0_.9, bf16[2,2,512,512]{3,2,1,0:T(8,128)(2,1)S(1)} %collective-permute-done.5.refs_1_, bf16[2,2,512,512]{3,2,1,0:T(8,128)(2,1)S(1)} %collective-permute-done.6.refs_2_, ...), custom_call_target="tpu_custom_call" | custom-call | flops 85899345920 | bytes 251658240 | tf_op jit(solution)/shard_map/pallas_call | solution.py:54
  88.5 0.0 reduce-scatter.4.cloned.1.call-update
  88.6 0.0 reduce-scatter.6.cloned.1.call-start
  88.6 2.5 constant_dynamic-slice_fusion.3
  91.1 1.5 pad_maximum_fusion.4
  92.6 0.0 collective-permute-start.9
  92.6 1.5 pad_maximum_fusion.5
  94.1 2.8 %collective-permute-start.10 = (bf16[2,2,512,512]{3,2,1,0:T(8,128)(2,1)}, bf16[2,2,512,512]{3,2,1,0:T(8,128)(2,1)}, u32[]{:S(2)}, u32[]{:S(2)}) collective-permute-start(bf16[2,2,512,512]{3,2,1,0:T(8,128)(2,1)} %pad_maximum_fusion.5), channel_id=1, source_target_pairs={{0,7},{1,0},{2,1},{3,2},{4,3},{5,4},{6,5},{7,6},{8,15},{9,8},{10,9... | collective-permute-start | bytes 6291464 | tf_op jit(solution)/shard_map/ppermute | solution.py:150
  96.9 27.4 %collective-permute-done.7.refs_1_ = bf16[2,2,512,512]{3,2,1,0:T(8,128)(2,1)S(1)} collective-permute-done((bf16[2,2,512,512]{3,2,1,0:T(8,128)(2,1)}, bf16[2,2,512,512]{3,2,1,0:T(8,128)(2,1)S(1)}, u32[]{:S(2)}, u32[]{:S(2)}) %collective-permute-start.7) | collective-permute-done | bytes 2097184 | tf_op jit(solution)/shard_map/ppermute | solution.py:149
  124.4 0.7 collective-permute-done.8.refs_2_
  125.1 8.7 %shard_map.57 = bf16[4,2,2,128,512]{4,3,2,1,0:T(8,128)(2,1)} custom-call(s32[4]{0:T(128)S(1)} %get-tuple-element.33.flags, s32[8]{0:T(128)S(1)} %copy-done.1, bf16[2,8,512,512]{3,2,1,0:T(8,128)(2,1)} %refs_0_.9, bf16[2,2,512,512]{3,2,1,0:T(8,128)(2,1)S(1)} %collective-permute-done.7.refs_1_, bf16[2,2,512,512]{3,2,1,0:T(8,128)(2,1)} %collective-permute-done.8.refs_2_, ...), custom_call_target="tpu_custom_call" | custom-call | flops 85899345920 | bytes 251658240 | tf_op jit(solution)/shard_map/pallas_call | solution.py:54
  133.8 0.0 reduce-scatter.6.cloned.1.call-update
  133.8 0.0 reduce-scatter.8.cloned.1.call-start
  133.9 2.7 %constant_dynamic-slice_fusion = (bf16[2,1,512,512]{3,2,1,0:T(8,128)(2,1)S(1)}, bf16[2,1,512,512]{3,2,1,0:T(8,128)(2,1)}) fusion(bf16[2,8,512,512]{3,2,1,0:T(8,128)(2,1)} %refs_0_.9, s32[]{:T(128)S(6)} %min.64, s32[]{:T(128)S(6)} %min.63), kind=kLoop, calls=%fused_computation.28 | loop fusion | bytes 4194312 | tf_op jit(solution)/shard_map/dynamic_slice | solution.py:111
  136.6 0.0 collective-permute-start.11
  136.6 3.1 %collective-permute-start.12 = (bf16[2,1,512,512]{3,2,1,0:T(8,128)(2,1)S(1)}, bf16[2,1,512,512]{3,2,1,0:T(8,128)(2,1)S(1)}, u32[]{:S(2)}, u32[]{:S(2)}) collective-permute-start(bf16[2,1,512,512]{3,2,1,0:T(8,128)(2,1)S(1)} %get-tuple-element.13), channel_id=1, source_target_pairs={{0,7},{1,0},{2,1},{3,2},{4,3},{5,4},{6,5},{7,6},{8,15},{9,8},{10,9... | collective-permute-start | bytes 3145736 | tf_op jit(solution)/shard_map/ppermute | solution.py:150
  139.7 29.7 %collective-permute-done.9.refs_1_ = bf16[2,2,512,512]{3,2,1,0:T(8,128)(2,1)} collective-permute-done((bf16[2,2,512,512]{3,2,1,0:T(8,128)(2,1)}, bf16[2,2,512,512]{3,2,1,0:T(8,128)(2,1)}, u32[]{:S(2)}, u32[]{:S(2)}) %collective-permute-start.9) | collective-permute-done | bytes 2097184 | tf_op jit(solution)/shard_map/ppermute | solution.py:149
  169.4 0.6 collective-permute-done.10.refs_2_
  170.1 9.0 %shard_map.58 = bf16[4,2,2,128,512]{4,3,2,1,0:T(8,128)(2,1)} custom-call(s32[4]{0:T(128)S(1)} %get-tuple-element.33.flags, s32[8]{0:T(128)S(1)} %copy-done.1, bf16[2,8,512,512]{3,2,1,0:T(8,128)(2,1)} %refs_0_.9, bf16[2,2,512,512]{3,2,1,0:T(8,128)(2,1)} %collective-permute-done.9.refs_1_, bf16[2,2,512,512]{3,2,1,0:T(8,128)(2,1)} %collective-permute-done.10.refs_2_, ...), custom_call_target="tpu_custom_call" | custom-call | flops 85899345920 | bytes 251658240 | tf_op jit(solution)/shard_map/pallas_call | solution.py:54
  179.1 0.0 reduce-scatter.8.cloned.1.call-update
  179.1 12.7 %collective-permute-done.11.refs_1_ = bf16[2,1,512,512]{3,2,1,0:T(8,128)(2,1)S(1)} collective-permute-done((bf16[2,1,512,512]{3,2,1,0:T(8,128)(2,1)}, bf16[2,1,512,512]{3,2,1,0:T(8,128)(2,1)S(1)}, u32[]{:S(2)}, u32[]{:S(2)}) %collective-permute-start.11) | collective-permute-done | bytes 1048608 | tf_op jit(solution)/shard_map/ppermute | solution.py:149
  191.8 3.4 %copy-done = bf16[2,8,512,512]{3,2,1,0:T(8,128)(2,1)S(1)} copy-done((bf16[2,8,512,512]{3,2,1,0:T(8,128)(2,1)S(1)}, bf16[2,8,512,512]{3,2,1,0:T(8,128)(2,1)}, u32[]{:S(2)}) %copy-start) | copy-done | bytes 8388632
  195.2 4.6 %shard_map.59 = bf16[4,2,1,128,512]{4,3,2,1,0:T(8,128)(2,1)S(1)} custom-call(s32[4]{0:T(128)S(1)} %get-tuple-element.33.flags, s32[8]{0:T(128)S(1)} %copy-done.1, bf16[2,8,512,512]{3,2,1,0:T(8,128)(2,1)S(1)} %copy-done, bf16[2,1,512,512]{3,2,1,0:T(8,128)(2,1)S(1)} %collective-permute-done.11.refs_1_, ...), custom_call_target="tpu_custom_call" | custom-call | flops 42949672960 | bytes 125829120 | tf_op jit(solution)/shard_map/pallas_call | solution.py:54
  199.9 0.1 dynamic-slice_bitcast_fusion.2
  200.0 1.4 collective-permute-start.15
  201.4 1.3 collective-permute-start.14
  202.7 1.9 collective-permute-start.13
  204.6 1.9 bitcast_dynamic-update-slice_fusion.2
  206.5 1.9 bitcast_dynamic-update-slice_fusion.1
  208.4 32.6 %reduce-scatter.8.cloned.1.call-done = bf16[1,2,2,128,512]{4,3,2,1,0:T(8,128)(2,1)} async-done(((bf16[4,2,2,128,512]{4,3,2,1,0:T(8,128)(2,1)}), bf16[1,2,2,128,512]{4,3,2,1,0:T(8,128)(2,1)}) %reduce-scatter.8.cloned.1.call-update) | async-done | bytes 524304 | tf_op jit(solution)/shard_map/reduce_scatter | solution.py:159
  241.0 1.9 bitcast_dynamic-update-slice_fusion
  242.9 0.0 collective-permute-done.15
  242.9 2.7 %collective-permute-done.14 = bf16[2,1,128,512]{3,2,0,1:T(8,128)(2,1)S(1)} collective-permute-done((bf16[2,1,128,512]{3,2,0,1:T(8,128)(2,1)S(1)}, bf16[2,1,128,512]{3,2,0,1:T(8,128)(2,1)S(1)}, u32[]{:S(2)}, u32[]{:S(2)}) %collective-permute-start.14) | collective-permute-done | bytes 262176 | tf_op jit(solution)/shard_map/ppermute | solution.py:118
  245.6 0.8 fusion.8
  (14 shorter events, 0.0 us)
Async XLA Ops:
  6.5 198.1 %reduce-scatter.4.cloned.1.call-start = ((), (), s32[]{:S(2)}) async-start(), calls=%async_computation.3 | async-start | bytes 2621440 | tf_op jit(solution)/shard_map/reduce_scatter | solution.py:159
  8.2 15.9 %collective-permute-start = (bf16[2,1,512,512]{3,2,1,0:T(8,128)(2,1)S(1)}, bf16[2,1,512,512]{3,2,1,0:T(8,128)(2,1)S(1)}, u32[]{:S(2)}, u32[]{:S(2)}) collective-permute-start(bf16[2,1,512,512]{3,2,1,0:T(8,128)(2,1)S(1)} %broadcast_select_fusion), channel_id=1, source_target_pairs={{0,1},{1,2},{2,3},{3,4},{4,5},{5,6},{6,7},{7,0},{8,15},{9,8},{10,9... | collective-permute-start | bytes 3145736 | tf_op jit(solution)/shard_map/ppermute | solution.py:138
  8.7 19.4 %copy-start.2 = (s32[2]{0:T(128)S(1)}, s32[2]{0:T(128)}, u32[]{:S(2)}) copy-start(s32[2]{0:T(128)} %param.9) | copy-start | bytes 28
  26.7 14.0 %collective-permute-start.1 = (bf16[2,1,512,512]{3,2,1,0:T(8,128)(2,1)}, bf16[2,1,512,512]{3,2,1,0:T(8,128)(2,1)S(1)}, u32[]{:S(2)}, u32[]{:S(2)}) collective-permute-start(bf16[2,1,512,512]{3,2,1,0:T(8,128)(2,1)} %select_select_fusion), channel_id=1, source_target_pairs={{0,8},{1,0},{2,10},{3,2},{4,12},{5,4},{6,14},{7,6},{8,9},{9,1},{10... | collective-permute-start | bytes 3145736 | tf_op jit(solution)/shard_map/ppermute | solution.py:145
  28.2 12.6 %slice-start = ((s8[8388608]{0:T(1024)(128)(4,1)}), s8[4194304]{0:T(1024)(128)(4,1)S(1)}, s32[]{:S(2)}) async-start(s8[8388608]{0:T(1024)(128)(4,1)} %bitcast.29), calls=%async_computation.6 | async-start | bytes 8388608
  30.8 9.9 %slice-start.1 = ((s8[8388608]{0:T(1024)(128)(4,1)}), s8[4194304]{0:T(1024)(128)(4,1)S(1)}, s32[]{:S(2)}) async-start(s8[8388608]{0:T(1024)(128)(4,1)} %bitcast.29), calls=%async_computation.7 | async-start | bytes 8388608
  31.0 48.4 %collective-permute-start.5 = (bf16[2,2,512,512]{3,2,1,0:T(8,128)(2,1)S(1)}, bf16[2,2,512,512]{3,2,1,0:T(8,128)(2,1)S(1)}, u32[]{:S(2)}, u32[]{:S(2)}) collective-permute-start(bf16[2,2,512,512]{3,2,1,0:T(8,128)(2,1)S(1)} %pad_maximum_fusion), channel_id=1, source_target_pairs={{0,1},{1,2},{2,3},{3,4},{4,5},{5,6},{6,7},{7,0},{8,9},{9,10},{10,1... | collective-permute-start | bytes 6291464 | tf_op jit(solution)/shard_map/ppermute | solution.py:149
  31.1 9.7 %copy-start.1 = (s32[8]{0:T(128)S(1)}, s32[8]{0:T(128)}, u32[]{:S(2)}) copy-start(s32[8]{0:T(128)} %dims.9) | copy-start | bytes 100
  31.3 48.8 %collective-permute-start.6 = (bf16[2,2,512,512]{3,2,1,0:T(8,128)(2,1)S(1)}, bf16[2,2,512,512]{3,2,1,0:T(8,128)(2,1)S(1)}, u32[]{:S(2)}, u32[]{:S(2)}) collective-permute-start(bf16[2,2,512,512]{3,2,1,0:T(8,128)(2,1)S(1)} %pad_maximum_fusion.1), channel_id=1, source_target_pairs={{0,7},{1,0},{2,1},{3,2},{4,3},{5,4},{6,5},{7,6},{8,15},{9,8},{10,9... | collective-permute-start | bytes 6291464 | tf_op jit(solution)/shard_map/ppermute | solution.py:150
  45.4 11.2 %collective-permute-start.4 = (bf16[2,1,128,512]{3,2,1,0:T(8,128)(2,1)S(1)}, bf16[2,1,128,512]{3,2,1,0:T(8,128)(2,1)S(1)}, u32[]{:S(2)}, u32[]{:S(2)}) collective-permute-start(bf16[2,1,128,512]{3,2,1,0:T(8,128)(2,1)S(1)} %get-tuple-element.31), channel_id=1, source_target_pairs={{0,24},{8,0},{16,8},{24,16},{1,25},{9,1},{17,9},{25,17},{2,26},{10... | collective-permute-start | bytes 786440 | tf_op jit(solution)/shard_map/ppermute | solution.py:118
  49.9 21.2 %collective-permute-start.3 = (bf16[2,1,128,512]{3,2,1,0:T(8,128)(2,1)S(1)}, bf16[2,1,128,512]{3,2,1,0:T(8,128)(2,1)S(1)}, u32[]{:S(2)}, u32[]{:S(2)}) collective-permute-start(bf16[2,1,128,512]{3,2,1,0:T(8,128)(2,1)S(1)} %get-tuple-element.32), channel_id=1, source_target_pairs={{0,16},{8,24},{16,0},{24,8},{1,17},{9,25},{17,1},{25,9},{2,18},{10... | collective-permute-start | bytes 786440 | tf_op jit(solution)/shard_map/ppermute | solution.py:118
  49.9 23.9 %collective-permute-start.2 = (bf16[2,1,128,512]{3,2,1,0:T(8,128)(2,1)S(1)}, bf16[2,1,128,512]{3,2,1,0:T(8,128)(2,1)S(1)}, u32[]{:S(2)}, u32[]{:S(2)}) collective-permute-start(bf16[2,1,128,512]{3,2,1,0:T(8,128)(2,1)S(1)} %get-tuple-element.30), channel_id=1, source_target_pairs={{0,8},{8,16},{16,24},{24,0},{1,9},{9,17},{17,25},{25,1},{2,10},{10... | collective-permute-start | bytes 786440 | tf_op jit(solution)/shard_map/ppermute | solution.py:118
  56.7 67.7 %collective-permute-start.7 = (bf16[2,2,512,512]{3,2,1,0:T(8,128)(2,1)}, bf16[2,2,512,512]{3,2,1,0:T(8,128)(2,1)S(1)}, u32[]{:S(2)}, u32[]{:S(2)}) collective-permute-start(bf16[2,2,512,512]{3,2,1,0:T(8,128)(2,1)} %pad_maximum_fusion.2), channel_id=1, source_target_pairs={{0,1},{1,2},{2,3},{3,4},{4,5},{5,6},{6,7},{7,0},{8,9},{9,10},{10,1... | collective-permute-start | bytes 6291464 | tf_op jit(solution)/shard_map/ppermute | solution.py:149
  71.1 54.0 %collective-permute-start.8 = (bf16[2,2,512,512]{3,2,1,0:T(8,128)(2,1)}, bf16[2,2,512,512]{3,2,1,0:T(8,128)(2,1)}, u32[]{:S(2)}, u32[]{:S(2)}) collective-permute-start(bf16[2,2,512,512]{3,2,1,0:T(8,128)(2,1)} %pad_maximum_fusion.3), channel_id=1, source_target_pairs={{0,7},{1,0},{2,1},{3,2},{4,3},{5,4},{6,5},{7,6},{8,15},{9,8},{10,9... | collective-permute-start | bytes 6291464 | tf_op jit(solution)/shard_map/ppermute | solution.py:150
  88.6 117.9 %reduce-scatter.6.cloned.1.call-start = ((), (), s32[]{:S(2)}) async-start(), calls=%async_computation.4 | async-start | bytes 2621440 | tf_op jit(solution)/shard_map/reduce_scatter | solution.py:159
  92.6 76.8 %collective-permute-start.9 = (bf16[2,2,512,512]{3,2,1,0:T(8,128)(2,1)}, bf16[2,2,512,512]{3,2,1,0:T(8,128)(2,1)}, u32[]{:S(2)}, u32[]{:S(2)}) collective-permute-start(bf16[2,2,512,512]{3,2,1,0:T(8,128)(2,1)} %pad_maximum_fusion.4), channel_id=1, source_target_pairs={{0,1},{1,2},{2,3},{3,4},{4,5},{5,6},{6,7},{7,0},{8,9},{9,10},{10,1... | collective-permute-start | bytes 6291464 | tf_op jit(solution)/shard_map/ppermute | solution.py:149
  94.1 75.9 %collective-permute-start.10 = (bf16[2,2,512,512]{3,2,1,0:T(8,128)(2,1)}, bf16[2,2,512,512]{3,2,1,0:T(8,128)(2,1)}, u32[]{:S(2)}, u32[]{:S(2)}) collective-permute-start(bf16[2,2,512,512]{3,2,1,0:T(8,128)(2,1)} %pad_maximum_fusion.5), channel_id=1, source_target_pairs={{0,7},{1,0},{2,1},{3,2},{4,3},{5,4},{6,5},{7,6},{8,15},{9,8},{10,9... | collective-permute-start | bytes 6291464 | tf_op jit(solution)/shard_map/ppermute | solution.py:150
  133.8 107.2 %reduce-scatter.8.cloned.1.call-start = ((), (), s32[]{:S(2)}) async-start(), calls=%async_computation.5 | async-start | bytes 2621440 | tf_op jit(solution)/shard_map/reduce_scatter | solution.py:159
  136.6 55.2 %collective-permute-start.11 = (bf16[2,1,512,512]{3,2,1,0:T(8,128)(2,1)}, bf16[2,1,512,512]{3,2,1,0:T(8,128)(2,1)S(1)}, u32[]{:S(2)}, u32[]{:S(2)}) collective-permute-start(bf16[2,1,512,512]{3,2,1,0:T(8,128)(2,1)} %get-tuple-element.14), channel_id=1, source_target_pairs={{0,1},{1,2},{2,3},{3,4},{4,5},{5,6},{6,7},{7,0},{8,9},{9,10},{10,1... | collective-permute-start | bytes 3145736 | tf_op jit(solution)/shard_map/ppermute | solution.py:149
  136.6 55.2 %collective-permute-start.12 = (bf16[2,1,512,512]{3,2,1,0:T(8,128)(2,1)S(1)}, bf16[2,1,512,512]{3,2,1,0:T(8,128)(2,1)S(1)}, u32[]{:S(2)}, u32[]{:S(2)}) collective-permute-start(bf16[2,1,512,512]{3,2,1,0:T(8,128)(2,1)S(1)} %get-tuple-element.13), channel_id=1, source_target_pairs={{0,7},{1,0},{2,1},{3,2},{4,3},{5,4},{6,5},{7,6},{8,15},{9,8},{10,9... | collective-permute-start | bytes 3145736 | tf_op jit(solution)/shard_map/ppermute | solution.py:150
  191.8 3.4 %copy-start = (bf16[2,8,512,512]{3,2,1,0:T(8,128)(2,1)S(1)}, bf16[2,8,512,512]{3,2,1,0:T(8,128)(2,1)}, u32[]{:S(2)}) copy-start(bf16[2,8,512,512]{3,2,1,0:T(8,128)(2,1)} %refs_0_.9) | copy-start | bytes 25165828
  200.0 42.9 %collective-permute-start.15 = (bf16[2,1,128,512]{3,2,0,1:T(8,128)(2,1)S(1)}, bf16[2,1,128,512]{3,2,0,1:T(8,128)(2,1)S(1)}, u32[]{:S(2)}, u32[]{:S(2)}) collective-permute-start(bf16[2,1,128,512]{3,2,0,1:T(8,128)(2,1)S(1)} %get-tuple-element.28), channel_id=1, source_target_pairs={{0,24},{8,0},{16,8},{24,16},{1,25},{9,1},{17,9},{25,17},{2,26},{10... | collective-permute-start | bytes 786440 | tf_op jit(solution)/shard_map/ppermute | solution.py:118
  201.4 44.1 %collective-permute-start.14 = (bf16[2,1,128,512]{3,2,0,1:T(8,128)(2,1)S(1)}, bf16[2,1,128,512]{3,2,0,1:T(8,128)(2,1)S(1)}, u32[]{:S(2)}, u32[]{:S(2)}) collective-permute-start(bf16[2,1,128,512]{3,2,0,1:T(8,128)(2,1)S(1)} %get-tuple-element.29), channel_id=1, source_target_pairs={{0,16},{8,24},{16,0},{24,8},{1,17},{9,25},{17,1},{25,9},{2,18},{10... | collective-permute-start | bytes 786440 | tf_op jit(solution)/shard_map/ppermute | solution.py:118
  202.7 42.9 %collective-permute-start.13 = (bf16[2,1,128,512]{3,2,0,1:T(8,128)(2,1)S(1)}, bf16[2,1,128,512]{3,2,0,1:T(8,128)(2,1)S(1)}, u32[]{:S(2)}, u32[]{:S(2)}) collective-permute-start(bf16[2,1,128,512]{3,2,0,1:T(8,128)(2,1)S(1)} %get-tuple-element.27), channel_id=1, source_target_pairs={{0,8},{8,16},{16,24},{24,0},{1,9},{9,17},{17,25},{25,1},{2,10},{10... | collective-permute-start | bytes 786440 | tf_op jit(solution)/shard_map/ppermute | solution.py:118
Sparse Core Ops, SparseCore 0:
  88.7 44.4 reduce-scatter.3
  135.6 43.1 reduce-scatter.5
  181.2 59.8 reduce-scatter.7

commit v3 on v2

--- a/solution.py
+++ b/solution.py
@@ -105,11 +105,17 @@
     can_share = planes % 2 == 0 and sec_count % 2 == 0
 
     def picked(source, first, count, offset):
-        parts = []
-        for slot in range(first, first + count):
-            at = jnp.clip(slot + offset, 0, slots - 1)
-            parts.append(lax.dynamic_slice_in_dim(source, at, 1, 1))
-        return jnp.concatenate(parts, axis=1)
+        step = -1 if offset is is_last else 1
+        parts = [
+            lax.slice_in_dim(source, at, at + 1, axis=1)
+            for at in (min(max(slot + step, 0), slots - 1) for slot in range(first, first + count))
+        ]
+        plain = lax.slice_in_dim(source, first, first + count, axis=1)
+        if 0 <= first + step and first + step + count <= slots:
+            moved = lax.slice_in_dim(source, first + step, first + step + count, axis=1)
+        else:
+            moved = jnp.concatenate(parts, axis=1)
+        return jnp.where(offset > 0, moved, plain)
 
     def sent_sum(partial):
         total = lax.dynamic_index_in_dim(partial, plane, 0, keepdims=False).astype(jnp.float32)
@@ -133,7 +139,7 @@
         elif len(partials) >= 2:
             source, _ = lax.optimization_barrier((source, partials[-2]))
         if fetch == "A" and can_share:
-            to_upper = picked(source, first, count, -is_last)
+            to_upper = picked(source, first, count, is_last)
             to_lower = picked(source, first, count, is_first)
             fetched = lax.ppermute(
                 jnp.where(odd == 0, to_upper, to_lower), ("mpo", "sec"), both
@@ -146,7 +152,7 @@
             )
             flags = shared_flags
         else:
-            from_lower = lax.ppermute(picked(source, first, count, -is_last), "sec", upward)
+            from_lower = lax.ppermute(picked(source, first, count, is_last), "sec", upward)
             from_upper = lax.ppermute(picked(source, first, count, is_first), "sec", downward)
             moved = (from_lower, from_upper)
             arrived.append(moved)

time: 253 us -> 253 us (level)
  local copies, waits for them, and re-layouts: 17.3 us -> 9.22 us
  other arithmetic: 12.5 us -> 18.7 us
    select_n x0 -> x3, other arithmetic: none -> 10.9 us  [picked(): return jnp.where(offset > 0, moved, plain)]
    dynamic_slice x4 -> x0, local copies, waits for them, and re-layouts: 8.08 us -> none  [picked(): parts.append(lax.dynamic_slice_in_dim(source, at, 1, 1))]
    concatenate x6 -> x0, other arithmetic: 6.4 us -> none  [picked(): return jnp.concatenate(parts, axis=1)]
    slice x0 -> x1, other arithmetic: none -> 2.7 us  [picked(): plain = lax.slice_in_dim(source, first, first + count, axis=1)]
    unnamed x13 -> x11, local copies, waits for them, and re-layouts: 9.07 us -> 9.05 us
where the time goes in v3:
time: 253 us; the launch traced here: 252 us
  waiting for transfers between devices  153 us (60%)
  Pallas kernels  35.4 us (14%)
  starting transfers between devices  23.2 us (9%)
  other arithmetic  18.7 us (7%)
  between operations  13.2 us (5%)
  local copies, waits for them, and re-layouts  9.22 us (4%)
    ppermute x4, waiting for transfers between devices, body(): lax.ppermute(picked(source, first, count, is_last), 'sec', upward)  77.2 us
    pallas_call x5, Pallas kernels, apply_rows(): pl.pallas_call(functools.partial(apply_kernel, first_slot=first_slot, slo...  35.4 us
    reduce_scatter x3, waiting for transfers between devices, body(): pieces.append(lax.psum_scatter(partial, 'mpo', scatter_dimension=0))  32.2 us
    ppermute x6, waiting for transfers between devices, sent_sum(): lax.ppermute(lax.dynamic_index_in_dim(partial, target, 0, keepdims=False)...  20.9 us
    ppermute x1, waiting for transfers between devices, body(): lax.ppermute(jnp.where(odd == 0, to_upper, to_lower), ('mpo', 'sec'), both)  15.4 us
    ppermute x4, starting transfers between devices, body(): lax.ppermute(picked(source, first, count, is_first), 'sec', downward)  11.3 us
    select_n x3, other arithmetic, picked(): return jnp.where(offset > 0, moved, plain)  10.9 us
    ppermute x6, starting transfers between devices, sent_sum(): lax.ppermute(lax.dynamic_index_in_dim(partial, target, 0, keepdims=False)...  9.85 us
  transfers between devices with their start and end apart: 19, of which 13 were waited for; matrix products, arithmetic and copies ran while one was open for 8% of the time, Pallas kernels for 14%

profile of v3, /device:TPU:0, one launch (start us, length us, event | category | flops | bytes accessed | tf_op | source)
XLA Modules:
  0.0 252.3 jit_solution(6113164372702330003)
XLA Ops:
  6.5 0.0 reduce-scatter.4.cloned.1.call-start
  6.5 1.6 select_select_fusion.1
  8.2 0.5 collective-permute-start
  8.7 0.0 copy-start.3
  8.7 15.4 %collective-permute-done.refs_1_ = bf16[2,1,512,512]{3,2,1,0:T(8,128)(2,1)S(1)} collective-permute-done((bf16[2,1,512,512]{3,2,1,0:T(8,128)(2,1)S(1)}, bf16[2,1,512,512]{3,2,1,0:T(8,128)(2,1)S(1)}, u32[]{:S(2)}, u32[]{:S(2)}) %collective-permute-start) | collective-permute-done | bytes 1048608 | tf_op jit(solution)/shard_map/ppermute | solution.py:144
  24.1 1.7 fusion
  25.8 1.5 collective-permute-start.1
  27.2 0.0 copy-done.3
  27.2 0.1 pad_add_fusion.1
  27.3 0.0 copy-start
  27.3 3.3 %slice_select_fusion.4 = (bf16[2,2,512,512]{3,2,1,0:T(8,128)(2,1)S(1)}, bf16[2,2,512,512]{3,2,1,0:T(8,128)(2,1)S(1)}) fusion(bf16[2,8,512,512]{3,2,1,0:T(8,128)(2,1)} %refs_0_.9, pred[]{:T(512)S(6)} %gt.7, pred[]{:T(512)S(6)} %gt.8), kind=kLoop, calls=%fused_computation.4 | loop fusion | flops 2097152 | bytes 10485762 | tf_op jit(solution)/shard_map/jit(_where)/select_n | solution.py:118
  30.7 0.1 collective-permute-start.5
  30.7 2.6 %collective-permute-start.6 = (bf16[2,2,512,512]{3,2,1,0:T(8,128)(2,1)S(1)}, bf16[2,2,512,512]{3,2,1,0:T(8,128)(2,1)S(1)}, u32[]{:S(2)}, u32[]{:S(2)}) collective-permute-start(bf16[2,2,512,512]{3,2,1,0:T(8,128)(2,1)S(1)} %get-tuple-element.19), channel_id=1, source_target_pairs={{0,7},{1,0},{2,1},{3,2},{4,3},{5,4},{6,5},{7,6},{8,15},{9,8},{10,9... | collective-permute-start | bytes 6291464 | tf_op jit(solution)/shard_map/ppermute | solution.py:156
  33.4 6.2 %collective-permute-done.1.refs_2_ = bf16[2,1,512,512]{3,2,1,0:T(8,128)(2,1)S(1)} collective-permute-done((bf16[2,1,512,512]{3,2,1,0:T(8,128)(2,1)S(1)}, bf16[2,1,512,512]{3,2,1,0:T(8,128)(2,1)S(1)}, u32[]{:S(2)}, u32[]{:S(2)}) %collective-permute-start.1) | collective-permute-done | bytes 1048608 | tf_op jit(solution)/shard_map/ppermute | solution.py:151
  39.5 0.0 copy-done
  39.6 0.0 copy-done.2
  39.6 4.6 %shard_map.55 = bf16[4,2,1,128,512]{4,3,2,1,0:T(8,128)(2,1)S(1)} custom-call(s32[4]{0:T(128)S(1)} %get-tuple-element.28.flags, s32[8]{0:T(128)S(1)} %copy-done.2, bf16[2,8,512,512]{3,2,1,0:T(8,128)(2,1)S(1)} %copy-done, bf16[2,1,512,512]{3,2,1,0:T(8,128)(2,1)S(1)} %collective-permute-done.refs_1_, ...), custom_call_target="tpu_custom_call" | custom-call | flops 42949672960 | bytes 125829120 | tf_op jit(solution)/shard_map/pallas_call | solution.py:54
  44.2 0.1 dynamic-slice_bitcast_fusion.5
  44.3 4.6 %collective-permute-start.4 = (bf16[2,1,128,512]{3,2,1,0:T(8,128)(2,1)S(1)}, bf16[2,1,128,512]{3,2,1,0:T(8,128)(2,1)S(1)}, u32[]{:S(2)}, u32[]{:S(2)}) collective-permute-start(bf16[2,1,128,512]{3,2,1,0:T(8,128)(2,1)S(1)} %get-tuple-element.25), channel_id=1, source_target_pairs={{0,24},{8,0},{16,8},{24,16},{1,25},{9,1},{17,9},{25,17},{2,26},{10... | collective-permute-start | bytes 786440 | tf_op jit(solution)/shard_map/ppermute | solution.py:124
  48.8 0.0 collective-permute-start.3
  48.8 0.6 collective-permute-start.2
  49.5 2.3 slice_select_fusion.2
  51.8 3.8 %collective-permute-done.4 = bf16[2,1,128,512]{3,2,1,0:T(8,128)(2,1)S(1)} collective-permute-done((bf16[2,1,128,512]{3,2,1,0:T(8,128)(2,1)S(1)}, bf16[2,1,128,512]{3,2,1,0:T(8,128)(2,1)S(1)}, u32[]{:S(2)}, u32[]{:S(2)}) %collective-permute-start.4) | collective-permute-done | bytes 262176 | tf_op jit(solution)/shard_map/ppermute | solution.py:124
  55.6 0.0 collective-permute-start.7
  55.6 14.4 %collective-permute-done.3 = bf16[2,1,128,512]{3,2,1,0:T(8,128)(2,1)S(1)} collective-permute-done((bf16[2,1,128,512]{3,2,1,0:T(8,128)(2,1)S(1)}, bf16[2,1,128,512]{3,2,1,0:T(8,128)(2,1)S(1)}, u32[]{:S(2)}, u32[]{:S(2)}) %collective-permute-start.3) | collective-permute-done | bytes 262176 | tf_op jit(solution)/shard_map/ppermute | solution.py:124
  70.0 2.7 %collective-permute-start.8 = (bf16[2,2,512,512]{3,2,1,0:T(8,128)(2,1)}, bf16[2,2,512,512]{3,2,1,0:T(8,128)(2,1)}, u32[]{:S(2)}, u32[]{:S(2)}) collective-permute-start(bf16[2,2,512,512]{3,2,1,0:T(8,128)(2,1)} %get-tuple-element.17), channel_id=1, source_target_pairs={{0,7},{1,0},{2,1},{3,2},{4,3},{5,4},{6,5},{7,6},{8,15},{9,8},{10,9... | collective-permute-start | bytes 6291464 | tf_op jit(solution)/shard_map/ppermute | solution.py:156
  72.7 0.0 collective-permute-done.2
  72.8 0.8 fusion.7
  73.6 5.7 %collective-permute-done.5.refs_1_ = bf16[2,2,512,512]{3,2,1,0:T(8,128)(2,1)S(1)} collective-permute-done((bf16[2,2,512,512]{3,2,1,0:T(8,128)(2,1)S(1)}, bf16[2,2,512,512]{3,2,1,0:T(8,128)(2,1)S(1)}, u32[]{:S(2)}, u32[]{:S(2)}) %collective-permute-start.5) | collective-permute-done | bytes 2097184 | tf_op jit(solution)/shard_map/ppermute | solution.py:155
  79.3 0.2 collective-permute-done.6.refs_2_
  79.5 8.4 %shard_map.56 = bf16[4,2,2,128,512]{4,3,2,1,0:T(8,128)(2,1)} custom-call(s32[4]{0:T(128)S(1)} %get-tuple-element.27.flags, s32[8]{0:T(128)S(1)} %copy-done.2, bf16[2,8,512,512]{3,2,1,0:T(8,128)(2,1)} %refs_0_.9, bf16[2,2,512,512]{3,2,1,0:T(8,128)(2,1)S(1)} %collective-permute-done.5.refs_1_, bf16[2,2,512,512]{3,2,1,0:T(8,128)(2,1)S(1)} %collective-permute-done.6.refs_2_, ...), custom_call_target="tpu_custom_call" | custom-call | flops 85899345920 | bytes 251658240 | tf_op jit(solution)/shard_map/pallas_call | solution.py:54
  87.8 0.0 reduce-scatter.4.cloned.1.call-update
  87.9 0.0 reduce-scatter.6.cloned.1.call-start
  87.9 5.3 %slice_select_fusion = (bf16[2,2,512,512]{3,2,1,0:T(8,128)(2,1)}, bf16[2,2,512,512]{3,2,1,0:T(8,128)(2,1)}) fusion(bf16[2,8,512,512]{3,2,1,0:T(8,128)(2,1)} %refs_0_.9, pred[]{:T(512)S(6)} %gt.7, pred[]{:T(512)S(6)} %gt.8), kind=kLoop, calls=%fused_computation | loop fusion | flops 2097152 | bytes 10485762 | tf_op jit(solution)/shard_map/jit(_where)/select_n | solution.py:118
  93.2 0.0 collective-permute-start.9
  93.2 2.8 %collective-permute-start.10 = (bf16[2,2,512,512]{3,2,1,0:T(8,128)(2,1)}, bf16[2,2,512,512]{3,2,1,0:T(8,128)(2,1)}, u32[]{:S(2)}, u32[]{:S(2)}) collective-permute-start(bf16[2,2,512,512]{3,2,1,0:T(8,128)(2,1)} %get-tuple-element.15), channel_id=1, source_target_pairs={{0,7},{1,0},{2,1},{3,2},{4,3},{5,4},{6,5},{7,6},{8,15},{9,8},{10,9... | collective-permute-start | bytes 6291464 | tf_op jit(solution)/shard_map/ppermute | solution.py:156
  96.0 28.2 %collective-permute-done.7.refs_1_ = bf16[2,2,512,512]{3,2,1,0:T(8,128)(2,1)S(1)} collective-permute-done((bf16[2,2,512,512]{3,2,1,0:T(8,128)(2,1)}, bf16[2,2,512,512]{3,2,1,0:T(8,128)(2,1)S(1)}, u32[]{:S(2)}, u32[]{:S(2)}) %collective-permute-start.7) | collective-permute-done | bytes 2097184 | tf_op jit(solution)/shard_map/ppermute | solution.py:155
  124.2 0.3 collective-permute-done.8.refs_2_
  124.5 8.7 %shard_map.57 = bf16[4,2,2,128,512]{4,3,2,1,0:T(8,128)(2,1)} custom-call(s32[4]{0:T(128)S(1)} %get-tuple-element.27.flags, s32[8]{0:T(128)S(1)} %copy-done.2, bf16[2,8,512,512]{3,2,1,0:T(8,128)(2,1)} %refs_0_.9, bf16[2,2,512,512]{3,2,1,0:T(8,128)(2,1)S(1)} %collective-permute-done.7.refs_1_, bf16[2,2,512,512]{3,2,1,0:T(8,128)(2,1)} %collective-permute-done.8.refs_2_, ...), custom_call_target="tpu_custom_call" | custom-call | flops 85899345920 | bytes 251658240 | tf_op jit(solution)/shard_map/pallas_call | solution.py:54
  133.2 0.0 reduce-scatter.6.cloned.1.call-update
  133.3 0.0 reduce-scatter.8.cloned.1.call-start
  133.3 2.7 %fusion.12 = (bf16[2,1,512,512]{3,2,1,0:T(8,128)(2,1)S(1)}, bf16[2,1,512,512]{3,2,1,0:T(8,128)(2,1)}) fusion(bf16[2,8,512,512]{3,2,1,0:T(8,128)(2,1)} %refs_0_.9, pred[]{:T(512)S(6)} %gt.8), kind=kLoop, calls=%fused_computation.39 | loop fusion | flops 524288 | bytes 4194305 | tf_op jit(solution)/shard_map/slice | solution.py:113
  136.0 0.0 collective-permute-start.11
  136.0 3.1 %collective-permute-start.12 = (bf16[2,1,512,512]{3,2,1,0:T(8,128)(2,1)S(1)}, bf16[2,1,512,512]{3,2,1,0:T(8,128)(2,1)S(1)}, u32[]{:S(2)}, u32[]{:S(2)}) collective-permute-start(bf16[2,1,512,512]{3,2,1,0:T(8,128)(2,1)S(1)} %get-tuple-element.13), channel_id=1, source_target_pairs={{0,7},{1,0},{2,1},{3,2},{4,3},{5,4},{6,5},{7,6},{8,15},{9,8},{10,9... | collective-permute-start | bytes 3145736 | tf_op jit(solution)/shard_map/ppermute | solution.py:156
  139.1 30.2 %collective-permute-done.9.refs_1_ = bf16[2,2,512,512]{3,2,1,0:T(8,128)(2,1)} collective-permute-done((bf16[2,2,512,512]{3,2,1,0:T(8,128)(2,1)}, bf16[2,2,512,512]{3,2,1,0:T(8,128)(2,1)}, u32[]{:S(2)}, u32[]{:S(2)}) %collective-permute-start.9) | collective-permute-done | bytes 2097184 | tf_op jit(solution)/shard_map/ppermute | solution.py:155
  169.3 0.2 collective-permute-done.10.refs_2_
  169.4 9.0 %shard_map.58 = bf16[4,2,2,128,512]{4,3,2,1,0:T(8,128)(2,1)} custom-call(s32[4]{0:T(128)S(1)} %get-tuple-element.27.flags, s32[8]{0:T(128)S(1)} %copy-done.2, bf16[2,8,512,512]{3,2,1,0:T(8,128)(2,1)} %refs_0_.9, bf16[2,2,512,512]{3,2,1,0:T(8,128)(2,1)} %collective-permute-done.9.refs_1_, bf16[2,2,512,512]{3,2,1,0:T(8,128)(2,1)} %collective-permute-done.10.refs_2_, ...), custom_call_target="tpu_custom_call" | custom-call | flops 85899345920 | bytes 251658240 | tf_op jit(solution)/shard_map/pallas_call | solution.py:54
  178.5 0.0 reduce-scatter.8.cloned.1.call-update
  178.5 13.1 %collective-permute-done.11.refs_1_ = bf16[2,1,512,512]{3,2,1,0:T(8,128)(2,1)S(1)} collective-permute-done((bf16[2,1,512,512]{3,2,1,0:T(8,128)(2,1)}, bf16[2,1,512,512]{3,2,1,0:T(8,128)(2,1)S(1)}, u32[]{:S(2)}, u32[]{:S(2)}) %collective-permute-start.11) | collective-permute-done | bytes 1048608 | tf_op jit(solution)/shard_map/ppermute | solution.py:155
  191.6 0.0 collective-permute-done.12.refs_2_
  191.6 3.4 %copy-done.1 = bf16[2,8,512,512]{3,2,1,0:T(8,128)(2,1)S(1)} copy-done((bf16[2,8,512,512]{3,2,1,0:T(8,128)(2,1)S(1)}, bf16[2,8,512,512]{3,2,1,0:T(8,128)(2,1)}, u32[]{:S(2)}) %copy-start.1) | copy-done | bytes 8388632
  195.1 4.6 %shard_map.59 = bf16[4,2,1,128,512]{4,3,2,1,0:T(8,128)(2,1)S(1)} custom-call(s32[4]{0:T(128)S(1)} %get-tuple-element.27.flags, s32[8]{0:T(128)S(1)} %copy-done.2, bf16[2,8,512,512]{3,2,1,0:T(8,128)(2,1)S(1)} %copy-done.1, bf16[2,1,512,512]{3,2,1,0:T(8,128)(2,1)S(1)} %collective-permute-done.11.refs_1_, ...), custom_call_target="tpu_custom_call" | custom-call | flops 42949672960 | bytes 125829120 | tf_op jit(solution)/shard_map/pallas_call | solution.py:54
  199.7 0.1 dynamic-slice_bitcast_fusion.2
  199.8 1.3 collective-permute-start.15
  201.0 1.4 collective-permute-start.14
  202.5 1.9 collective-permute-start.13
  204.4 1.9 bitcast_dynamic-update-slice_fusion.2
  206.3 1.9 bitcast_dynamic-update-slice_fusion.1
  208.2 32.2 %reduce-scatter.8.cloned.1.call-done = bf16[1,2,2,128,512]{4,3,2,1,0:T(8,128)(2,1)} async-done(((bf16[4,2,2,128,512]{4,3,2,1,0:T(8,128)(2,1)}), bf16[1,2,2,128,512]{4,3,2,1,0:T(8,128)(2,1)}) %reduce-scatter.8.cloned.1.call-update) | async-done | bytes 524304 | tf_op jit(solution)/shard_map/reduce_scatter | solution.py:165
  240.3 1.9 bitcast_dynamic-update-slice_fusion
  242.2 0.0 collective-permute-done.15
  242.2 2.7 %collective-permute-done.14 = bf16[2,1,128,512]{3,2,0,1:T(8,128)(2,1)S(1)} collective-permute-done((bf16[2,1,128,512]{3,2,0,1:T(8,128)(2,1)S(1)}, bf16[2,1,128,512]{3,2,0,1:T(8,128)(2,1)S(1)}, u32[]{:S(2)}, u32[]{:S(2)}) %collective-permute-start.14) | collective-permute-done | bytes 262176 | tf_op jit(solution)/shard_map/ppermute | solution.py:124
  244.9 0.0 collective-permute-done.13
  244.9 0.8 fusion.9
  (5 shorter events, 0.0 us)
Async XLA Ops:
  6.5 197.9 %reduce-scatter.4.cloned.1.call-start = ((), (), s32[]{:S(2)}) async-start(), calls=%async_computation.3 | async-start | bytes 2621440 | tf_op jit(solution)/shard_map/reduce_scatter | solution.py:165
  8.2 15.9 %collective-permute-start = (bf16[2,1,512,512]{3,2,1,0:T(8,128)(2,1)S(1)}, bf16[2,1,512,512]{3,2,1,0:T(8,128)(2,1)S(1)}, u32[]{:S(2)}, u32[]{:S(2)}) collective-permute-start(bf16[2,1,512,512]{3,2,1,0:T(8,128)(2,1)S(1)} %select_select_fusion.1), channel_id=1, source_target_pairs={{0,1},{1,2},{2,3},{3,4},{4,5},{5,6},{6,7},{7,0},{8,15},{9,8},{10,9... | collective-permute-start | bytes 3145736 | tf_op jit(solution)/shard_map/ppermute | solution.py:144
  8.7 18.5 %copy-start.3 = (s32[2]{0:T(128)S(1)}, s32[2]{0:T(128)}, u32[]{:S(2)}) copy-start(s32[2]{0:T(128)} %param.9) | copy-start | bytes 28
  25.8 13.8 %collective-permute-start.1 = (bf16[2,1,512,512]{3,2,1,0:T(8,128)(2,1)S(1)}, bf16[2,1,512,512]{3,2,1,0:T(8,128)(2,1)S(1)}, u32[]{:S(2)}, u32[]{:S(2)}) collective-permute-start(bf16[2,1,512,512]{3,2,1,0:T(8,128)(2,1)S(1)} %fusion), channel_id=1, source_target_pairs={{0,8},{1,0},{2,10},{3,2},{4,12},{5,4},{6,14},{7,6},{8,9},{9,1},{10... | collective-permute-start | bytes 3145736 | tf_op jit(solution)/shard_map/ppermute | solution.py:151
  27.3 12.2 %copy-start = (bf16[2,8,512,512]{3,2,1,0:T(8,128)(2,1)S(1)}, bf16[2,8,512,512]{3,2,1,0:T(8,128)(2,1)}, u32[]{:S(2)}) copy-start(bf16[2,8,512,512]{3,2,1,0:T(8,128)(2,1)} %refs_0_.9) | copy-start | bytes 25165828
  27.3 12.2 %copy-start.2 = (s32[8]{0:T(128)S(1)}, s32[8]{0:T(128)}, u32[]{:S(2)}) copy-start(s32[8]{0:T(128)} %dims.9) | copy-start | bytes 100
  30.7 48.6 %collective-permute-start.5 = (bf16[2,2,512,512]{3,2,1,0:T(8,128)(2,1)S(1)}, bf16[2,2,512,512]{3,2,1,0:T(8,128)(2,1)S(1)}, u32[]{:S(2)}, u32[]{:S(2)}) collective-permute-start(bf16[2,2,512,512]{3,2,1,0:T(8,128)(2,1)S(1)} %get-tuple-element.20), channel_id=1, source_target_pairs={{0,1},{1,2},{2,3},{3,4},{4,5},{5,6},{6,7},{7,0},{8,9},{9,10},{10,1... | collective-permute-start | bytes 6291464 | tf_op jit(solution)/shard_map/ppermute | solution.py:155
  30.7 48.7 %collective-permute-start.6 = (bf16[2,2,512,512]{3,2,1,0:T(8,128)(2,1)S(1)}, bf16[2,2,512,512]{3,2,1,0:T(8,128)(2,1)S(1)}, u32[]{:S(2)}, u32[]{:S(2)}) collective-permute-start(bf16[2,2,512,512]{3,2,1,0:T(8,128)(2,1)S(1)} %get-tuple-element.19), channel_id=1, source_target_pairs={{0,7},{1,0},{2,1},{3,2},{4,3},{5,4},{6,5},{7,6},{8,15},{9,8},{10,9... | collective-permute-start | bytes 6291464 | tf_op jit(solution)/shard_map/ppermute | solution.py:156
  44.3 11.3 %collective-permute-start.4 = (bf16[2,1,128,512]{3,2,1,0:T(8,128)(2,1)S(1)}, bf16[2,1,128,512]{3,2,1,0:T(8,128)(2,1)S(1)}, u32[]{:S(2)}, u32[]{:S(2)}) collective-permute-start(bf16[2,1,128,512]{3,2,1,0:T(8,128)(2,1)S(1)} %get-tuple-element.25), channel_id=1, source_target_pairs={{0,24},{8,0},{16,8},{24,16},{1,25},{9,1},{17,9},{25,17},{2,26},{10... | collective-permute-start | bytes 786440 | tf_op jit(solution)/shard_map/ppermute | solution.py:124
  48.8 21.2 %collective-permute-start.3 = (bf16[2,1,128,512]{3,2,1,0:T(8,128)(2,1)S(1)}, bf16[2,1,128,512]{3,2,1,0:T(8,128)(2,1)S(1)}, u32[]{:S(2)}, u32[]{:S(2)}) collective-permute-start(bf16[2,1,128,512]{3,2,1,0:T(8,128)(2,1)S(1)} %get-tuple-element.26), channel_id=1, source_target_pairs={{0,16},{8,24},{16,0},{24,8},{1,17},{9,25},{17,1},{25,9},{2,18},{10... | collective-permute-start | bytes 786440 | tf_op jit(solution)/shard_map/ppermute | solution.py:124
  48.8 23.9 %collective-permute-start.2 = (bf16[2,1,128,512]{3,2,1,0:T(8,128)(2,1)S(1)}, bf16[2,1,128,512]{3,2,1,0:T(8,128)(2,1)S(1)}, u32[]{:S(2)}, u32[]{:S(2)}) collective-permute-start(bf16[2,1,128,512]{3,2,1,0:T(8,128)(2,1)S(1)} %get-tuple-element.24), channel_id=1, source_target_pairs={{0,8},{8,16},{16,24},{24,0},{1,9},{9,17},{17,25},{25,1},{2,10},{10... | collective-permute-start | bytes 786440 | tf_op jit(solution)/shard_map/ppermute | solution.py:124
  55.6 68.6 %collective-permute-start.7 = (bf16[2,2,512,512]{3,2,1,0:T(8,128)(2,1)}, bf16[2,2,512,512]{3,2,1,0:T(8,128)(2,1)S(1)}, u32[]{:S(2)}, u32[]{:S(2)}) collective-permute-start(bf16[2,2,512,512]{3,2,1,0:T(8,128)(2,1)} %get-tuple-element.18), channel_id=1, source_target_pairs={{0,1},{1,2},{2,3},{3,4},{4,5},{5,6},{6,7},{7,0},{8,9},{9,10},{10,1... | collective-permute-start | bytes 6291464 | tf_op jit(solution)/shard_map/ppermute | solution.py:155
  70.0 54.5 %collective-permute-start.8 = (bf16[2,2,512,512]{3,2,1,0:T(8,128)(2,1)}, bf16[2,2,512,512]{3,2,1,0:T(8,128)(2,1)}, u32[]{:S(2)}, u32[]{:S(2)}) collective-permute-start(bf16[2,2,512,512]{3,2,1,0:T(8,128)(2,1)} %get-tuple-element.17), channel_id=1, source_target_pairs={{0,7},{1,0},{2,1},{3,2},{4,3},{5,4},{6,5},{7,6},{8,15},{9,8},{10,9... | collective-permute-start | bytes 6291464 | tf_op jit(solution)/shard_map/ppermute | solution.py:156
  87.9 118.4 %reduce-scatter.6.cloned.1.call-start = ((), (), s32[]{:S(2)}) async-start(), calls=%async_computation.4 | async-start | bytes 2621440 | tf_op jit(solution)/shard_map/reduce_scatter | solution.py:165
  93.2 76.1 %collective-permute-start.9 = (bf16[2,2,512,512]{3,2,1,0:T(8,128)(2,1)}, bf16[2,2,512,512]{3,2,1,0:T(8,128)(2,1)}, u32[]{:S(2)}, u32[]{:S(2)}) collective-permute-start(bf16[2,2,512,512]{3,2,1,0:T(8,128)(2,1)} %get-tuple-element.16), channel_id=1, source_target_pairs={{0,1},{1,2},{2,3},{3,4},{4,5},{5,6},{6,7},{7,0},{8,9},{9,10},{10,1... | collective-permute-start | bytes 6291464 | tf_op jit(solution)/shard_map/ppermute | solution.py:155
  93.2 76.3 %collective-permute-start.10 = (bf16[2,2,512,512]{3,2,1,0:T(8,128)(2,1)}, bf16[2,2,512,512]{3,2,1,0:T(8,128)(2,1)}, u32[]{:S(2)}, u32[]{:S(2)}) collective-permute-start(bf16[2,2,512,512]{3,2,1,0:T(8,128)(2,1)} %get-tuple-element.15), channel_id=1, source_target_pairs={{0,7},{1,0},{2,1},{3,2},{4,3},{5,4},{6,5},{7,6},{8,15},{9,8},{10,9... | collective-permute-start | bytes 6291464 | tf_op jit(solution)/shard_map/ppermute | solution.py:156
  133.3 107.1 %reduce-scatter.8.cloned.1.call-start = ((), (), s32[]{:S(2)}) async-start(), calls=%async_computation.5 | async-start | bytes 2621440 | tf_op jit(solution)/shard_map/reduce_scatter | solution.py:165
  136.0 55.6 %collective-permute-start.11 = (bf16[2,1,512,512]{3,2,1,0:T(8,128)(2,1)}, bf16[2,1,512,512]{3,2,1,0:T(8,128)(2,1)S(1)}, u32[]{:S(2)}, u32[]{:S(2)}) collective-permute-start(bf16[2,1,512,512]{3,2,1,0:T(8,128)(2,1)} %get-tuple-element.14), channel_id=1, source_target_pairs={{0,1},{1,2},{2,3},{3,4},{4,5},{5,6},{6,7},{7,0},{8,9},{9,10},{10,1... | collective-permute-start | bytes 3145736 | tf_op jit(solution)/shard_map/ppermute | solution.py:155
  136.0 55.6 %collective-permute-start.12 = (bf16[2,1,512,512]{3,2,1,0:T(8,128)(2,1)S(1)}, bf16[2,1,512,512]{3,2,1,0:T(8,128)(2,1)S(1)}, u32[]{:S(2)}, u32[]{:S(2)}) collective-permute-start(bf16[2,1,512,512]{3,2,1,0:T(8,128)(2,1)S(1)} %get-tuple-element.13), channel_id=1, source_target_pairs={{0,7},{1,0},{2,1},{3,2},{4,3},{5,4},{6,5},{7,6},{8,15},{9,8},{10,9... | collective-permute-start | bytes 3145736 | tf_op jit(solution)/shard_map/ppermute | solution.py:156
  191.6 3.4 %copy-start.1 = (bf16[2,8,512,512]{3,2,1,0:T(8,128)(2,1)S(1)}, bf16[2,8,512,512]{3,2,1,0:T(8,128)(2,1)}, u32[]{:S(2)}) copy-start(bf16[2,8,512,512]{3,2,1,0:T(8,128)(2,1)} %refs_0_.9) | copy-start | bytes 25165828
  199.8 42.4 %collective-permute-start.15 = (bf16[2,1,128,512]{3,2,0,1:T(8,128)(2,1)S(1)}, bf16[2,1,128,512]{3,2,0,1:T(8,128)(2,1)S(1)}, u32[]{:S(2)}, u32[]{:S(2)}) collective-permute-start(bf16[2,1,128,512]{3,2,0,1:T(8,128)(2,1)S(1)} %get-tuple-element.22), channel_id=1, source_target_pairs={{0,24},{8,0},{16,8},{24,16},{1,25},{9,1},{17,9},{25,17},{2,26},{10... | collective-permute-start | bytes 786440 | tf_op jit(solution)/shard_map/ppermute | solution.py:124
  201.0 43.9 %collective-permute-start.14 = (bf16[2,1,128,512]{3,2,0,1:T(8,128)(2,1)S(1)}, bf16[2,1,128,512]{3,2,0,1:T(8,128)(2,1)S(1)}, u32[]{:S(2)}, u32[]{:S(2)}) collective-permute-start(bf16[2,1,128,512]{3,2,0,1:T(8,128)(2,1)S(1)} %get-tuple-element.23), channel_id=1, source_target_pairs={{0,16},{8,24},{16,0},{24,8},{1,17},{9,25},{17,1},{25,9},{2,18},{10... | collective-permute-start | bytes 786440 | tf_op jit(solution)/shard_map/ppermute | solution.py:124
  202.5 42.4 %collective-permute-start.13 = (bf16[2,1,128,512]{3,2,0,1:T(8,128)(2,1)S(1)}, bf16[2,1,128,512]{3,2,0,1:T(8,128)(2,1)S(1)}, u32[]{:S(2)}, u32[]{:S(2)}) collective-permute-start(bf16[2,1,128,512]{3,2,0,1:T(8,128)(2,1)S(1)} %get-tuple-element.21), channel_id=1, source_target_pairs={{0,8},{8,16},{16,24},{24,0},{1,9},{9,17},{17,25},{25,1},{2,10},{10... | collective-permute-start | bytes 786440 | tf_op jit(solution)/shard_map/ppermute | solution.py:124
Sparse Core Ops, SparseCore 0:
  88.0 44.4 reduce-scatter.3
  134.9 43.1 reduce-scatter.5
  180.5 59.8 reduce-scatter.7

commit v4 on v3

--- a/solution.py
+++ b/solution.py
@@ -23,7 +23,7 @@
     col_index = lax.broadcasted_iota(jnp.int32, (size, size), 1)
     inside = jnp.logical_and(row_index < limit, col_index < limit)
     for k in range(vectors):
-        total = jnp.zeros((size, size), jnp.float32)
+        parts = []
         for row in range(rows):
             pick, edge = flags[row], flags[rows + row]
             live = jnp.logical_not(
@@ -37,9 +37,12 @@
                 chosen = jnp.where(pick == i, sources[i][k, 0], chosen)
             chosen = jnp.where(live, chosen, jnp.zeros_like(chosen))
             part = jnp.dot(left[row, 0], chosen, preferred_element_type=jnp.float32)
-            total += jnp.dot(
-                part.astype(jnp.bfloat16), right[row, 0], preferred_element_type=jnp.float32
-            )
+            parts.append(part.astype(jnp.bfloat16))
+        total = jnp.dot(
+            jnp.concatenate(parts, axis=1),
+            right[:, 0].reshape(rows * size, size),
+            preferred_element_type=jnp.float32,
+        )
         kept = jnp.where(inside, total, jnp.zeros_like(total)).astype(out.dtype)
         for chunk in range(chunks):
             out[chunk, k, 0] = kept[chunk * slab : (chunk + 1) * slab]

time: 253 us -> 253 us (level)
  no operation moved by 1% of the time
where the time goes in v4:
time: 253 us; the launch traced here: 252 us
  waiting for transfers between devices  153 us (60%)
  Pallas kernels  35.4 us (14%)
  starting transfers between devices  23.2 us (9%)
  other arithmetic  18.7 us (7%)
  between operations  13.2 us (5%)
  local copies, waits for them, and re-layouts  9.22 us (4%)
    ppermute x4, waiting for transfers between devices, body(): lax.ppermute(picked(source, first, count, is_last), 'sec', upward)  77.2 us
    pallas_call x5, Pallas kernels, apply_rows(): pl.pallas_call(functools.partial(apply_kernel, first_slot=first_slot, slo...  35.4 us
    reduce_scatter x3, waiting for transfers between devices, body(): pieces.append(lax.psum_scatter(partial, 'mpo', scatter_dimension=0))  32.2 us
    ppermute x6, waiting for transfers between devices, sent_sum(): lax.ppermute(lax.dynamic_index_in_dim(partial, target, 0, keepdims=False)...  20.9 us
    ppermute x1, waiting for transfers between devices, body(): lax.ppermute(jnp.where(odd == 0, to_upper, to_lower), ('mpo', 'sec'), both)  15.4 us
    ppermute x4, starting transfers between devices, body(): lax.ppermute(picked(source, first, count, is_first), 'sec', downward)  11.3 us
    select_n x3, other arithmetic, picked(): return jnp.where(offset > 0, moved, plain)  10.9 us
    ppermute x6, starting transfers between devices, sent_sum(): lax.ppermute(lax.dynamic_index_in_dim(partial, target, 0, keepdims=False)...  9.85 us
  transfers between devices with their start and end apart: 19, of which 13 were waited for; matrix products, arithmetic and copies ran while one was open for 8% of the time, Pallas kernels for 14%

profile of v4, /device:TPU:0, one launch (start us, length us, event | category | flops | bytes accessed | tf_op | source)
XLA Modules:
  0.0 252.3 jit_solution(2942744831277637755)
XLA Ops:
  6.5 0.0 reduce-scatter.4.cloned.1.call-start
  6.5 1.6 select_select_fusion.1
  8.2 0.5 collective-permute-start
  8.7 0.0 copy-start.3
  8.7 15.4 %collective-permute-done.refs_1_ = bf16[2,1,512,512]{3,2,1,0:T(8,128)(2,1)S(1)} collective-permute-done((bf16[2,1,512,512]{3,2,1,0:T(8,128)(2,1)S(1)}, bf16[2,1,512,512]{3,2,1,0:T(8,128)(2,1)S(1)}, u32[]{:S(2)}, u32[]{:S(2)}) %collective-permute-start) | collective-permute-done | bytes 1048608 | tf_op jit(solution)/shard_map/ppermute | solution.py:147
  24.1 1.7 fusion
  25.8 1.5 collective-permute-start.1
  27.2 0.0 copy-done.3
  27.2 0.1 pad_add_fusion.1
  27.3 0.0 copy-start
  27.3 3.3 %slice_select_fusion.4 = (bf16[2,2,512,512]{3,2,1,0:T(8,128)(2,1)S(1)}, bf16[2,2,512,512]{3,2,1,0:T(8,128)(2,1)S(1)}) fusion(bf16[2,8,512,512]{3,2,1,0:T(8,128)(2,1)} %refs_0_.9, pred[]{:T(512)S(6)} %gt.7, pred[]{:T(512)S(6)} %gt.8), kind=kLoop, calls=%fused_computation.4 | loop fusion | flops 2097152 | bytes 10485762 | tf_op jit(solution)/shard_map/jit(_where)/select_n | solution.py:121
  30.7 0.1 collective-permute-start.5
  30.7 2.6 %collective-permute-start.6 = (bf16[2,2,512,512]{3,2,1,0:T(8,128)(2,1)S(1)}, bf16[2,2,512,512]{3,2,1,0:T(8,128)(2,1)S(1)}, u32[]{:S(2)}, u32[]{:S(2)}) collective-permute-start(bf16[2,2,512,512]{3,2,1,0:T(8,128)(2,1)S(1)} %get-tuple-element.19), channel_id=1, source_target_pairs={{0,7},{1,0},{2,1},{3,2},{4,3},{5,4},{6,5},{7,6},{8,15},{9,8},{10,9... | collective-permute-start | bytes 6291464 | tf_op jit(solution)/shard_map/ppermute | solution.py:159
  33.4 6.2 %collective-permute-done.1.refs_2_ = bf16[2,1,512,512]{3,2,1,0:T(8,128)(2,1)S(1)} collective-permute-done((bf16[2,1,512,512]{3,2,1,0:T(8,128)(2,1)S(1)}, bf16[2,1,512,512]{3,2,1,0:T(8,128)(2,1)S(1)}, u32[]{:S(2)}, u32[]{:S(2)}) %collective-permute-start.1) | collective-permute-done | bytes 1048608 | tf_op jit(solution)/shard_map/ppermute | solution.py:154
  39.5 0.0 copy-done
  39.6 0.0 copy-done.2
  39.6 4.6 %shard_map.55 = bf16[4,2,1,128,512]{4,3,2,1,0:T(8,128)(2,1)S(1)} custom-call(s32[4]{0:T(128)S(1)} %get-tuple-element.28.flags, s32[8]{0:T(128)S(1)} %copy-done.2, bf16[2,8,512,512]{3,2,1,0:T(8,128)(2,1)S(1)} %copy-done, bf16[2,1,512,512]{3,2,1,0:T(8,128)(2,1)S(1)} %collective-permute-done.refs_1_, ...), custom_call_target="tpu_custom_call" | custom-call | flops 42949672960 | bytes 125829120 | tf_op jit(solution)/shard_map/pallas_call | solution.py:57
  44.2 0.1 dynamic-slice_bitcast_fusion.5
  44.3 4.6 %collective-permute-start.4 = (bf16[2,1,128,512]{3,2,1,0:T(8,128)(2,1)S(1)}, bf16[2,1,128,512]{3,2,1,0:T(8,128)(2,1)S(1)}, u32[]{:S(2)}, u32[]{:S(2)}) collective-permute-start(bf16[2,1,128,512]{3,2,1,0:T(8,128)(2,1)S(1)} %get-tuple-element.25), channel_id=1, source_target_pairs={{0,24},{8,0},{16,8},{24,16},{1,25},{9,1},{17,9},{25,17},{2,26},{10... | collective-permute-start | bytes 786440 | tf_op jit(solution)/shard_map/ppermute | solution.py:127
  48.8 0.0 collective-permute-start.3
  48.8 0.6 collective-permute-start.2
  49.5 2.3 slice_select_fusion.2
  51.8 3.8 %collective-permute-done.4 = bf16[2,1,128,512]{3,2,1,0:T(8,128)(2,1)S(1)} collective-permute-done((bf16[2,1,128,512]{3,2,1,0:T(8,128)(2,1)S(1)}, bf16[2,1,128,512]{3,2,1,0:T(8,128)(2,1)S(1)}, u32[]{:S(2)}, u32[]{:S(2)}) %collective-permute-start.4) | collective-permute-done | bytes 262176 | tf_op jit(solution)/shard_map/ppermute | solution.py:127
  55.6 0.0 collective-permute-start.7
  55.6 14.4 %collective-permute-done.3 = bf16[2,1,128,512]{3,2,1,0:T(8,128)(2,1)S(1)} collective-permute-done((bf16[2,1,128,512]{3,2,1,0:T(8,128)(2,1)S(1)}, bf16[2,1,128,512]{3,2,1,0:T(8,128)(2,1)S(1)}, u32[]{:S(2)}, u32[]{:S(2)}) %collective-permute-start.3) | collective-permute-done | bytes 262176 | tf_op jit(solution)/shard_map/ppermute | solution.py:127
  70.0 2.7 %collective-permute-start.8 = (bf16[2,2,512,512]{3,2,1,0:T(8,128)(2,1)}, bf16[2,2,512,512]{3,2,1,0:T(8,128)(2,1)}, u32[]{:S(2)}, u32[]{:S(2)}) collective-permute-start(bf16[2,2,512,512]{3,2,1,0:T(8,128)(2,1)} %get-tuple-element.17), channel_id=1, source_target_pairs={{0,7},{1,0},{2,1},{3,2},{4,3},{5,4},{6,5},{7,6},{8,15},{9,8},{10,9... | collective-permute-start | bytes 6291464 | tf_op jit(solution)/shard_map/ppermute | solution.py:159
  72.8 0.0 collective-permute-done.2
  72.8 0.8 fusion.7
  73.6 5.7 %collective-permute-done.5.refs_1_ = bf16[2,2,512,512]{3,2,1,0:T(8,128)(2,1)S(1)} collective-permute-done((bf16[2,2,512,512]{3,2,1,0:T(8,128)(2,1)S(1)}, bf16[2,2,512,512]{3,2,1,0:T(8,128)(2,1)S(1)}, u32[]{:S(2)}, u32[]{:S(2)}) %collective-permute-start.5) | collective-permute-done | bytes 2097184 | tf_op jit(solution)/shard_map/ppermute | solution.py:158
  79.3 0.2 collective-permute-done.6.refs_2_
  79.5 8.4 %shard_map.56 = bf16[4,2,2,128,512]{4,3,2,1,0:T(8,128)(2,1)} custom-call(s32[4]{0:T(128)S(1)} %get-tuple-element.27.flags, s32[8]{0:T(128)S(1)} %copy-done.2, bf16[2,8,512,512]{3,2,1,0:T(8,128)(2,1)} %refs_0_.9, bf16[2,2,512,512]{3,2,1,0:T(8,128)(2,1)S(1)} %collective-permute-done.5.refs_1_, bf16[2,2,512,512]{3,2,1,0:T(8,128)(2,1)S(1)} %collective-permute-done.6.refs_2_, ...), custom_call_target="tpu_custom_call" | custom-call | flops 85899345920 | bytes 251658240 | tf_op jit(solution)/shard_map/pallas_call | solution.py:57
  87.9 0.0 reduce-scatter.4.cloned.1.call-update
  87.9 0.0 reduce-scatter.6.cloned.1.call-start
  87.9 5.3 %slice_select_fusion = (bf16[2,2,512,512]{3,2,1,0:T(8,128)(2,1)}, bf16[2,2,512,512]{3,2,1,0:T(8,128)(2,1)}) fusion(bf16[2,8,512,512]{3,2,1,0:T(8,128)(2,1)} %refs_0_.9, pred[]{:T(512)S(6)} %gt.7, pred[]{:T(512)S(6)} %gt.8), kind=kLoop, calls=%fused_computation | loop fusion | flops 2097152 | bytes 10485762 | tf_op jit(solution)/shard_map/jit(_where)/select_n | solution.py:121
  93.2 0.0 collective-permute-start.9
  93.2 2.8 %collective-permute-start.10 = (bf16[2,2,512,512]{3,2,1,0:T(8,128)(2,1)}, bf16[2,2,512,512]{3,2,1,0:T(8,128)(2,1)}, u32[]{:S(2)}, u32[]{:S(2)}) collective-permute-start(bf16[2,2,512,512]{3,2,1,0:T(8,128)(2,1)} %get-tuple-element.15), channel_id=1, source_target_pairs={{0,7},{1,0},{2,1},{3,2},{4,3},{5,4},{6,5},{7,6},{8,15},{9,8},{10,9... | collective-permute-start | bytes 6291464 | tf_op jit(solution)/shard_map/ppermute | solution.py:159
  96.0 28.2 %collective-permute-done.7.refs_1_ = bf16[2,2,512,512]{3,2,1,0:T(8,128)(2,1)S(1)} collective-permute-done((bf16[2,2,512,512]{3,2,1,0:T(8,128)(2,1)}, bf16[2,2,512,512]{3,2,1,0:T(8,128)(2,1)S(1)}, u32[]{:S(2)}, u32[]{:S(2)}) %collective-permute-start.7) | collective-permute-done | bytes 2097184 | tf_op jit(solution)/shard_map/ppermute | solution.py:158
  124.2 0.3 collective-permute-done.8.refs_2_
  124.5 8.7 %shard_map.57 = bf16[4,2,2,128,512]{4,3,2,1,0:T(8,128)(2,1)} custom-call(s32[4]{0:T(128)S(1)} %get-tuple-element.27.flags, s32[8]{0:T(128)S(1)} %copy-done.2, bf16[2,8,512,512]{3,2,1,0:T(8,128)(2,1)} %refs_0_.9, bf16[2,2,512,512]{3,2,1,0:T(8,128)(2,1)S(1)} %collective-permute-done.7.refs_1_, bf16[2,2,512,512]{3,2,1,0:T(8,128)(2,1)} %collective-permute-done.8.refs_2_, ...), custom_call_target="tpu_custom_call" | custom-call | flops 85899345920 | bytes 251658240 | tf_op jit(solution)/shard_map/pallas_call | solution.py:57
  133.2 0.0 reduce-scatter.6.cloned.1.call-update
  133.3 0.0 reduce-scatter.8.cloned.1.call-start
  133.3 2.7 %fusion.12 = (bf16[2,1,512,512]{3,2,1,0:T(8,128)(2,1)S(1)}, bf16[2,1,512,512]{3,2,1,0:T(8,128)(2,1)}) fusion(bf16[2,8,512,512]{3,2,1,0:T(8,128)(2,1)} %refs_0_.9, pred[]{:T(512)S(6)} %gt.8), kind=kLoop, calls=%fused_computation.39 | loop fusion | flops 524288 | bytes 4194305 | tf_op jit(solution)/shard_map/slice | solution.py:116
  136.0 0.0 collective-permute-start.11
  136.0 3.1 %collective-permute-start.12 = (bf16[2,1,512,512]{3,2,1,0:T(8,128)(2,1)S(1)}, bf16[2,1,512,512]{3,2,1,0:T(8,128)(2,1)S(1)}, u32[]{:S(2)}, u32[]{:S(2)}) collective-permute-start(bf16[2,1,512,512]{3,2,1,0:T(8,128)(2,1)S(1)} %get-tuple-element.13), channel_id=1, source_target_pairs={{0,7},{1,0},{2,1},{3,2},{4,3},{5,4},{6,5},{7,6},{8,15},{9,8},{10,9... | collective-permute-start | bytes 3145736 | tf_op jit(solution)/shard_map/ppermute | solution.py:159
  139.1 30.2 %collective-permute-done.9.refs_1_ = bf16[2,2,512,512]{3,2,1,0:T(8,128)(2,1)} collective-permute-done((bf16[2,2,512,512]{3,2,1,0:T(8,128)(2,1)}, bf16[2,2,512,512]{3,2,1,0:T(8,128)(2,1)}, u32[]{:S(2)}, u32[]{:S(2)}) %collective-permute-start.9) | collective-permute-done | bytes 2097184 | tf_op jit(solution)/shard_map/ppermute | solution.py:158
  169.3 0.2 collective-permute-done.10.refs_2_
  169.4 9.0 %shard_map.58 = bf16[4,2,2,128,512]{4,3,2,1,0:T(8,128)(2,1)} custom-call(s32[4]{0:T(128)S(1)} %get-tuple-element.27.flags, s32[8]{0:T(128)S(1)} %copy-done.2, bf16[2,8,512,512]{3,2,1,0:T(8,128)(2,1)} %refs_0_.9, bf16[2,2,512,512]{3,2,1,0:T(8,128)(2,1)} %collective-permute-done.9.refs_1_, bf16[2,2,512,512]{3,2,1,0:T(8,128)(2,1)} %collective-permute-done.10.refs_2_, ...), custom_call_target="tpu_custom_call" | custom-call | flops 85899345920 | bytes 251658240 | tf_op jit(solution)/shard_map/pallas_call | solution.py:57
  178.5 0.0 reduce-scatter.8.cloned.1.call-update
  178.5 13.1 %collective-permute-done.11.refs_1_ = bf16[2,1,512,512]{3,2,1,0:T(8,128)(2,1)S(1)} collective-permute-done((bf16[2,1,512,512]{3,2,1,0:T(8,128)(2,1)}, bf16[2,1,512,512]{3,2,1,0:T(8,128)(2,1)S(1)}, u32[]{:S(2)}, u32[]{:S(2)}) %collective-permute-start.11) | collective-permute-done | bytes 1048608 | tf_op jit(solution)/shard_map/ppermute | solution.py:158
  191.6 0.0 collective-permute-done.12.refs_2_
  191.6 3.4 %copy-done.1 = bf16[2,8,512,512]{3,2,1,0:T(8,128)(2,1)S(1)} copy-done((bf16[2,8,512,512]{3,2,1,0:T(8,128)(2,1)S(1)}, bf16[2,8,512,512]{3,2,1,0:T(8,128)(2,1)}, u32[]{:S(2)}) %copy-start.1) | copy-done | bytes 8388632
  195.1 4.6 %shard_map.59 = bf16[4,2,1,128,512]{4,3,2,1,0:T(8,128)(2,1)S(1)} custom-call(s32[4]{0:T(128)S(1)} %get-tuple-element.27.flags, s32[8]{0:T(128)S(1)} %copy-done.2, bf16[2,8,512,512]{3,2,1,0:T(8,128)(2,1)S(1)} %copy-done.1, bf16[2,1,512,512]{3,2,1,0:T(8,128)(2,1)S(1)} %collective-permute-done.11.refs_1_, ...), custom_call_target="tpu_custom_call" | custom-call | flops 42949672960 | bytes 125829120 | tf_op jit(solution)/shard_map/pallas_call | solution.py:57
  199.7 0.1 dynamic-slice_bitcast_fusion.2
  199.8 1.2 collective-permute-start.15
  201.0 1.4 collective-permute-start.14
  202.5 1.9 collective-permute-start.13
  204.4 1.9 bitcast_dynamic-update-slice_fusion.2
  206.3 1.9 bitcast_dynamic-update-slice_fusion.1
  208.2 32.2 %reduce-scatter.8.cloned.1.call-done = bf16[1,2,2,128,512]{4,3,2,1,0:T(8,128)(2,1)} async-done(((bf16[4,2,2,128,512]{4,3,2,1,0:T(8,128)(2,1)}), bf16[1,2,2,128,512]{4,3,2,1,0:T(8,128)(2,1)}) %reduce-scatter.8.cloned.1.call-update) | async-done | bytes 524304 | tf_op jit(solution)/shard_map/reduce_scatter | solution.py:168
  240.3 1.9 bitcast_dynamic-update-slice_fusion
  242.2 0.0 collective-permute-done.15
  242.2 2.7 %collective-permute-done.14 = bf16[2,1,128,512]{3,2,0,1:T(8,128)(2,1)S(1)} collective-permute-done((bf16[2,1,128,512]{3,2,0,1:T(8,128)(2,1)S(1)}, bf16[2,1,128,512]{3,2,0,1:T(8,128)(2,1)S(1)}, u32[]{:S(2)}, u32[]{:S(2)}) %collective-permute-start.14) | collective-permute-done | bytes 262176 | tf_op jit(solution)/shard_map/ppermute | solution.py:127
  244.9 0.0 collective-permute-done.13
  244.9 0.8 fusion.9
  (5 shorter events, 0.0 us)
Async XLA Ops:
  6.5 197.9 %reduce-scatter.4.cloned.1.call-start = ((), (), s32[]{:S(2)}) async-start(), calls=%async_computation.3 | async-start | bytes 2621440 | tf_op jit(solution)/shard_map/reduce_scatter | solution.py:168
  8.2 15.9 %collective-permute-start = (bf16[2,1,512,512]{3,2,1,0:T(8,128)(2,1)S(1)}, bf16[2,1,512,512]{3,2,1,0:T(8,128)(2,1)S(1)}, u32[]{:S(2)}, u32[]{:S(2)}) collective-permute-start(bf16[2,1,512,512]{3,2,1,0:T(8,128)(2,1)S(1)} %select_select_fusion.1), channel_id=1, source_target_pairs={{0,1},{1,2},{2,3},{3,4},{4,5},{5,6},{6,7},{7,0},{8,15},{9,8},{10,9... | collective-permute-start | bytes 3145736 | tf_op jit(solution)/shard_map/ppermute | solution.py:147
  8.7 18.5 %copy-start.3 = (s32[2]{0:T(128)S(1)}, s32[2]{0:T(128)}, u32[]{:S(2)}) copy-start(s32[2]{0:T(128)} %param.9) | copy-start | bytes 28
  25.8 13.8 %collective-permute-start.1 = (bf16[2,1,512,512]{3,2,1,0:T(8,128)(2,1)S(1)}, bf16[2,1,512,512]{3,2,1,0:T(8,128)(2,1)S(1)}, u32[]{:S(2)}, u32[]{:S(2)}) collective-permute-start(bf16[2,1,512,512]{3,2,1,0:T(8,128)(2,1)S(1)} %fusion), channel_id=1, source_target_pairs={{0,8},{1,0},{2,10},{3,2},{4,12},{5,4},{6,14},{7,6},{8,9},{9,1},{10... | collective-permute-start | bytes 3145736 | tf_op jit(solution)/shard_map/ppermute | solution.py:154
  27.3 12.2 %copy-start = (bf16[2,8,512,512]{3,2,1,0:T(8,128)(2,1)S(1)}, bf16[2,8,512,512]{3,2,1,0:T(8,128)(2,1)}, u32[]{:S(2)}) copy-start(bf16[2,8,512,512]{3,2,1,0:T(8,128)(2,1)} %refs_0_.9) | copy-start | bytes 25165828
  27.3 12.2 %copy-start.2 = (s32[8]{0:T(128)S(1)}, s32[8]{0:T(128)}, u32[]{:S(2)}) copy-start(s32[8]{0:T(128)} %dims.9) | copy-start | bytes 100
  30.7 48.6 %collective-permute-start.5 = (bf16[2,2,512,512]{3,2,1,0:T(8,128)(2,1)S(1)}, bf16[2,2,512,512]{3,2,1,0:T(8,128)(2,1)S(1)}, u32[]{:S(2)}, u32[]{:S(2)}) collective-permute-start(bf16[2,2,512,512]{3,2,1,0:T(8,128)(2,1)S(1)} %get-tuple-element.20), channel_id=1, source_target_pairs={{0,1},{1,2},{2,3},{3,4},{4,5},{5,6},{6,7},{7,0},{8,9},{9,10},{10,1... | collective-permute-start | bytes 6291464 | tf_op jit(solution)/shard_map/ppermute | solution.py:158
  30.7 48.7 %collective-permute-start.6 = (bf16[2,2,512,512]{3,2,1,0:T(8,128)(2,1)S(1)}, bf16[2,2,512,512]{3,2,1,0:T(8,128)(2,1)S(1)}, u32[]{:S(2)}, u32[]{:S(2)}) collective-permute-start(bf16[2,2,512,512]{3,2,1,0:T(8,128)(2,1)S(1)} %get-tuple-element.19), channel_id=1, source_target_pairs={{0,7},{1,0},{2,1},{3,2},{4,3},{5,4},{6,5},{7,6},{8,15},{9,8},{10,9... | collective-permute-start | bytes 6291464 | tf_op jit(solution)/shard_map/ppermute | solution.py:159
  44.3 11.3 %collective-permute-start.4 = (bf16[2,1,128,512]{3,2,1,0:T(8,128)(2,1)S(1)}, bf16[2,1,128,512]{3,2,1,0:T(8,128)(2,1)S(1)}, u32[]{:S(2)}, u32[]{:S(2)}) collective-permute-start(bf16[2,1,128,512]{3,2,1,0:T(8,128)(2,1)S(1)} %get-tuple-element.25), channel_id=1, source_target_pairs={{0,24},{8,0},{16,8},{24,16},{1,25},{9,1},{17,9},{25,17},{2,26},{10... | collective-permute-start | bytes 786440 | tf_op jit(solution)/shard_map/ppermute | solution.py:127
  48.8 21.2 %collective-permute-start.3 = (bf16[2,1,128,512]{3,2,1,0:T(8,128)(2,1)S(1)}, bf16[2,1,128,512]{3,2,1,0:T(8,128)(2,1)S(1)}, u32[]{:S(2)}, u32[]{:S(2)}) collective-permute-start(bf16[2,1,128,512]{3,2,1,0:T(8,128)(2,1)S(1)} %get-tuple-element.26), channel_id=1, source_target_pairs={{0,16},{8,24},{16,0},{24,8},{1,17},{9,25},{17,1},{25,9},{2,18},{10... | collective-permute-start | bytes 786440 | tf_op jit(solution)/shard_map/ppermute | solution.py:127
  48.8 23.9 %collective-permute-start.2 = (bf16[2,1,128,512]{3,2,1,0:T(8,128)(2,1)S(1)}, bf16[2,1,128,512]{3,2,1,0:T(8,128)(2,1)S(1)}, u32[]{:S(2)}, u32[]{:S(2)}) collective-permute-start(bf16[2,1,128,512]{3,2,1,0:T(8,128)(2,1)S(1)} %get-tuple-element.24), channel_id=1, source_target_pairs={{0,8},{8,16},{16,24},{24,0},{1,9},{9,17},{17,25},{25,1},{2,10},{10... | collective-permute-start | bytes 786440 | tf_op jit(solution)/shard_map/ppermute | solution.py:127
  55.6 68.6 %collective-permute-start.7 = (bf16[2,2,512,512]{3,2,1,0:T(8,128)(2,1)}, bf16[2,2,512,512]{3,2,1,0:T(8,128)(2,1)S(1)}, u32[]{:S(2)}, u32[]{:S(2)}) collective-permute-start(bf16[2,2,512,512]{3,2,1,0:T(8,128)(2,1)} %get-tuple-element.18), channel_id=1, source_target_pairs={{0,1},{1,2},{2,3},{3,4},{4,5},{5,6},{6,7},{7,0},{8,9},{9,10},{10,1... | collective-permute-start | bytes 6291464 | tf_op jit(solution)/shard_map/ppermute | solution.py:158
  70.0 54.5 %collective-permute-start.8 = (bf16[2,2,512,512]{3,2,1,0:T(8,128)(2,1)}, bf16[2,2,512,512]{3,2,1,0:T(8,128)(2,1)}, u32[]{:S(2)}, u32[]{:S(2)}) collective-permute-start(bf16[2,2,512,512]{3,2,1,0:T(8,128)(2,1)} %get-tuple-element.17), channel_id=1, source_target_pairs={{0,7},{1,0},{2,1},{3,2},{4,3},{5,4},{6,5},{7,6},{8,15},{9,8},{10,9... | collective-permute-start | bytes 6291464 | tf_op jit(solution)/shard_map/ppermute | solution.py:159
  87.9 118.4 %reduce-scatter.6.cloned.1.call-start = ((), (), s32[]{:S(2)}) async-start(), calls=%async_computation.4 | async-start | bytes 2621440 | tf_op jit(solution)/shard_map/reduce_scatter | solution.py:168
  93.2 76.1 %collective-permute-start.9 = (bf16[2,2,512,512]{3,2,1,0:T(8,128)(2,1)}, bf16[2,2,512,512]{3,2,1,0:T(8,128)(2,1)}, u32[]{:S(2)}, u32[]{:S(2)}) collective-permute-start(bf16[2,2,512,512]{3,2,1,0:T(8,128)(2,1)} %get-tuple-element.16), channel_id=1, source_target_pairs={{0,1},{1,2},{2,3},{3,4},{4,5},{5,6},{6,7},{7,0},{8,9},{9,10},{10,1... | collective-permute-start | bytes 6291464 | tf_op jit(solution)/shard_map/ppermute | solution.py:158
  93.2 76.2 %collective-permute-start.10 = (bf16[2,2,512,512]{3,2,1,0:T(8,128)(2,1)}, bf16[2,2,512,512]{3,2,1,0:T(8,128)(2,1)}, u32[]{:S(2)}, u32[]{:S(2)}) collective-permute-start(bf16[2,2,512,512]{3,2,1,0:T(8,128)(2,1)} %get-tuple-element.15), channel_id=1, source_target_pairs={{0,7},{1,0},{2,1},{3,2},{4,3},{5,4},{6,5},{7,6},{8,15},{9,8},{10,9... | collective-permute-start | bytes 6291464 | tf_op jit(solution)/shard_map/ppermute | solution.py:159
  133.3 107.1 %reduce-scatter.8.cloned.1.call-start = ((), (), s32[]{:S(2)}) async-start(), calls=%async_computation.5 | async-start | bytes 2621440 | tf_op jit(solution)/shard_map/reduce_scatter | solution.py:168
  136.0 55.6 %collective-permute-start.11 = (bf16[2,1,512,512]{3,2,1,0:T(8,128)(2,1)}, bf16[2,1,512,512]{3,2,1,0:T(8,128)(2,1)S(1)}, u32[]{:S(2)}, u32[]{:S(2)}) collective-permute-start(bf16[2,1,512,512]{3,2,1,0:T(8,128)(2,1)} %get-tuple-element.14), channel_id=1, source_target_pairs={{0,1},{1,2},{2,3},{3,4},{4,5},{5,6},{6,7},{7,0},{8,9},{9,10},{10,1... | collective-permute-start | bytes 3145736 | tf_op jit(solution)/shard_map/ppermute | solution.py:158
  136.0 55.6 %collective-permute-start.12 = (bf16[2,1,512,512]{3,2,1,0:T(8,128)(2,1)S(1)}, bf16[2,1,512,512]{3,2,1,0:T(8,128)(2,1)S(1)}, u32[]{:S(2)}, u32[]{:S(2)}) collective-permute-start(bf16[2,1,512,512]{3,2,1,0:T(8,128)(2,1)S(1)} %get-tuple-element.13), channel_id=1, source_target_pairs={{0,7},{1,0},{2,1},{3,2},{4,3},{5,4},{6,5},{7,6},{8,15},{9,8},{10,9... | collective-permute-start | bytes 3145736 | tf_op jit(solution)/shard_map/ppermute | solution.py:159
  191.6 3.4 %copy-start.1 = (bf16[2,8,512,512]{3,2,1,0:T(8,128)(2,1)S(1)}, bf16[2,8,512,512]{3,2,1,0:T(8,128)(2,1)}, u32[]{:S(2)}) copy-start(bf16[2,8,512,512]{3,2,1,0:T(8,128)(2,1)} %refs_0_.9) | copy-start | bytes 25165828
  199.8 42.4 %collective-permute-start.15 = (bf16[2,1,128,512]{3,2,0,1:T(8,128)(2,1)S(1)}, bf16[2,1,128,512]{3,2,0,1:T(8,128)(2,1)S(1)}, u32[]{:S(2)}, u32[]{:S(2)}) collective-permute-start(bf16[2,1,128,512]{3,2,0,1:T(8,128)(2,1)S(1)} %get-tuple-element.22), channel_id=1, source_target_pairs={{0,24},{8,0},{16,8},{24,16},{1,25},{9,1},{17,9},{25,17},{2,26},{10... | collective-permute-start | bytes 786440 | tf_op jit(solution)/shard_map/ppermute | solution.py:127
  201.0 43.9 %collective-permute-start.14 = (bf16[2,1,128,512]{3,2,0,1:T(8,128)(2,1)S(1)}, bf16[2,1,128,512]{3,2,0,1:T(8,128)(2,1)S(1)}, u32[]{:S(2)}, u32[]{:S(2)}) collective-permute-start(bf16[2,1,128,512]{3,2,0,1:T(8,128)(2,1)S(1)} %get-tuple-element.23), channel_id=1, source_target_pairs={{0,16},{8,24},{16,0},{24,8},{1,17},{9,25},{17,1},{25,9},{2,18},{10... | collective-permute-start | bytes 786440 | tf_op jit(solution)/shard_map/ppermute | solution.py:127
  202.5 42.4 %collective-permute-start.13 = (bf16[2,1,128,512]{3,2,0,1:T(8,128)(2,1)S(1)}, bf16[2,1,128,512]{3,2,0,1:T(8,128)(2,1)S(1)}, u32[]{:S(2)}, u32[]{:S(2)}) collective-permute-start(bf16[2,1,128,512]{3,2,0,1:T(8,128)(2,1)S(1)} %get-tuple-element.21), channel_id=1, source_target_pairs={{0,8},{8,16},{16,24},{24,0},{1,9},{9,17},{17,25},{25,1},{2,10},{10... | collective-permute-start | bytes 786440 | tf_op jit(solution)/shard_map/ppermute | solution.py:127
Sparse Core Ops, SparseCore 0:
  88.0 44.4 reduce-scatter.3
  134.9 43.1 reduce-scatter.5
  180.5 59.8 reduce-scatter.7
